TPU v7x, 512 devices: a whole 4x4x16 slice. The times are simulated.
512 devices in a mesh: pair: 16 (over x_hi, y, core), row: 32 (over x_lo, z).
Axes of the slice: x: 4 (x_hi: 2, x_lo: 2; x = x_hi * 2 + x_lo), y: 4, z: 16, core: 2. Of those that a mesh axis runs over, the one named last changes fastest.
Arguments:
- snapshots: float32 [4096, 8192], P('row', 'pair'), may hold values from -60 to 60
Outputs:
- rotated: float32 [4096, 8192], P('row', 'pair')
All inputs are finite; a program needn't handle non-finite values.
Results may differ from a plain program's by a relative error of at most 0.0003.
Values sent between devices are 32-bit elements; how exact they have to be, the bound alone decides.
No kernel may reach another device: no remote copies, remote signals or barrier semaphores. Data moves between devices by JAX's collectives and lax.ppermute only.
A program may use at most 64 MiB of HBM per device.

v0:
```python
import jax
import jax.numpy as jnp
import numpy as np
from jax import lax
from jax.sharding import PartitionSpec as P

STEPS = 3
ROUNDS = 3


def shifted(x, axis, by):
    count = lax.axis_size(axis)
    pairs = [(i, i + by) for i in range(count) if 0 <= i + by < count]
    return lax.ppermute(x, axis, pairs)


def round_robin(order_size, section_count):
    players = list(range(order_size))
    orders = []
    half_size = order_size // 2
    for section_index in range(section_count):
        layout = [players[position_i] for position_i in range(half_size)] + [
            players[order_size - 1 - position_i] for position_i in range(half_size)
        ]
        orders.append(np.array(layout, dtype=np.int32))
        players = [players[0], players[-1]] + players[1:-1]
    return orders


def angles(current):
    half_size = current.shape[0] // 2
    diagonal = jnp.diagonal(current)
    upper_diag = diagonal[:half_size]
    lower_diag = diagonal[half_size:]
    coupling = jnp.diagonal(current[:half_size, half_size:])
    difference = lower_diag - upper_diag
    sign_term = jnp.where(difference >= 0, 1.0, -1.0)
    radius = jnp.sqrt(
        difference * difference
        + 4.0 * coupling * coupling
        + (1e-06 * (upper_diag + lower_diag)) ** 2
    )
    tangent = 2.0 * coupling * sign_term / (jnp.abs(difference) + radius)
    cosine = 1.0 / jnp.sqrt(1.0 + tangent * tangent)
    return (cosine, tangent * cosine)


def turn_rows(matrix, cosine, sine_term):
    half_size = matrix.shape[0] // 2
    leading = matrix[:half_size]
    second = matrix[half_size:]
    return jnp.concatenate(
        [
            cosine[:, None] * leading - sine_term[:, None] * second,
            sine_term[:, None] * leading + cosine[:, None] * second,
        ],
        axis=0,
    )


def turn_cols(matrix, cosine, sine_term):
    half_size = matrix.shape[1] // 2
    leading = matrix[:, :half_size]
    second = matrix[:, half_size:]
    return jnp.concatenate(
        [
            cosine[None, :] * leading - sine_term[None, :] * second,
            sine_term[None, :] * leading + cosine[None, :] * second,
        ],
        axis=1,
    )


def diagonalize(gram_matrix):
    order_size = gram_matrix.shape[0]
    orders = round_robin(order_size, STEPS)
    current = gram_matrix[orders[0]][:, orders[0]]
    frame_basis = jnp.eye(order_size, dtype=gram_matrix.dtype)[:, orders[0]]
    for sweep_step in range(STEPS):
        if sweep_step > 0:
            relative = np.argsort(orders[sweep_step - 1])[orders[sweep_step]]
            current = current[relative][:, relative]
            frame_basis = frame_basis[:, relative]
        cosine, sine_term = angles(current)
        current = turn_cols(turn_rows(current, cosine, sine_term), cosine, sine_term)
        frame_basis = turn_cols(frame_basis, cosine, sine_term)
    restore = np.argsort(orders[-1])
    return (frame_basis[:, restore], current[restore][:, restore])


def local_gram(upper_block, lower_block):
    joined = jnp.concatenate([upper_block, lower_block], axis=1)
    return jnp.einsum("ra,rb->ab", joined, joined, precision=lax.Precision.HIGHEST)


def first_total(upper_block, lower_block):
    return lax.psum(local_gram(upper_block, lower_block), "row")


def rotate_pair(upper_block, lower_block, frame_basis):
    joined = jnp.concatenate([upper_block, lower_block], axis=1)
    turned = jnp.dot(joined, frame_basis, precision=lax.Precision.HIGHEST)
    half_width = upper_block.shape[1]
    return (turned[:, :half_width], turned[:, half_width:])


def move_blocks(upper_block, lower_block):
    position = lax.axis_index("pair")
    pair_count = lax.axis_size("pair")
    outgoing = jnp.where(position == 0, lower_block, upper_block)
    arriving = shifted(outgoing, "pair", 1)
    departing = shifted(lower_block, "pair", -1)
    new_upper = jnp.where(position == 0, upper_block, arriving)
    new_lower = jnp.where(position == pair_count - 1, upper_block, departing)
    return (new_upper, new_lower)


def per_device(snapshots):
    half_width = snapshots.shape[1] // 2
    upper_block = snapshots[:, :half_width]
    lower_block = snapshots[:, half_width:]
    gram_matrix = first_total(upper_block, lower_block)
    for round_index in range(ROUNDS):
        if round_index > 0:
            gram_matrix = lax.psum(local_gram(upper_block, lower_block), "row")
        frame_basis, turned_gram = diagonalize(gram_matrix)
        upper_block, lower_block = rotate_pair(upper_block, lower_block, frame_basis)
        upper_block, lower_block = move_blocks(upper_block, lower_block)
    return jnp.concatenate([upper_block, lower_block], axis=1)


def solution(mesh):
    return jax.shard_map(
        per_device,
        mesh=mesh,
        in_specs=(P("row", "pair"),),
        out_specs=P("row", "pair"),
        check_vma=False,
    )
```

profile of v0, /device:TPU:25, one launch (start us, length us, event | category | flops | bytes accessed | tf_op | source)
XLA Modules:
  0.0 971.8 jit_solution(1014151825033708472)
XLA Ops:
  7.5 2.0 fusion.87
  13.4 238.0 %all-reduce.4.cloned.1.call-done = f32[512,512]{1,0:T(8,128)} async-done(((f32[512,512]{1,0:T(8,128)}), f32[512,512]{1,0:T(8,128)}) %all-reduce.4.cloned.1.call-update) | async-done | bytes 1048592 | tf_op jit(solution)/shard_map/psum | solution.py:97
  251.4 3.2 gather_fusion
  256.6 4.5 gather_fusion.3
  261.2 2.4 gather_fusion.2
  268.2 4.5 gather_fusion.7
  272.8 2.4 gather_fusion.6
  281.3 4.5 gather_fusion.11
  285.9 2.4 gather_fusion.10
  292.9 26.8 %collective-permute-start = (f32[128,256]{0,1:T(8,128)S(1)}, f32[128,256]{0,1:T(8,128)S(1)}, u32[]{:S(2)}, u32[]{:S(2)}) collective-permute-start(f32[128,256]{0,1:T(8,128)S(1)} %get-tuple-element.75), channel_id=1, source_target_pairs={{0,32},{32,64},{64,96},{96,128},{128,160},{160,192},{192,224},{224... | collective-permute-start | bytes 393224 | tf_op jit(solution)/shard_map/ppermute | solution.py:14
  321.6 8.0 collective-permute-done.1
  331.7 226.8 %all-reduce.6.cloned.1.call-done = f32[512,512]{1,0:T(8,128)} async-done(((f32[512,512]{1,0:T(8,128)}), f32[512,512]{1,0:T(8,128)}) %all-reduce.6.cloned.1.call-update) | async-done | bytes 1048592 | tf_op jit(solution)/shard_map/psum | solution.py:125
  558.5 12.5 %gather_fusion.16 = f32[512,512]{1,0:T(8,128)S(1)} fusion(f32[512,512]{1,0:T(8,128)} %all-reduce.6.cloned.1.call-done, s32[1024]{0:T(1024)S(1)} %pad_clamp_fusion.2), kind=kCustom, calls=%fused_computation.16 | custom fusion | bytes 2099200 | tf_op jit(solution)/shard_map/gather | solution.py:77
  573.0 4.5 gather_fusion.19
  577.6 2.4 gather_fusion.18
  586.6 4.5 gather_fusion.23
  591.2 2.4 gather_fusion.22
  594.8 2.3 gather_fusion.28
  603.7 4.5 gather_fusion.27
  608.3 2.4 gather_fusion.26
  616.9 26.8 %collective-permute-start.2 = (f32[128,256]{0,1:T(8,128)S(1)}, f32[128,256]{0,1:T(8,128)S(1)}, u32[]{:S(2)}, u32[]{:S(2)}) collective-permute-start(f32[128,256]{0,1:T(8,128)S(1)} %get-tuple-element.71), channel_id=1, source_target_pairs={{0,32},{32,64},{64,96},{96,128},{128,160},{160,192},{192,224},{224... | collective-permute-start | bytes 393224 | tf_op jit(solution)/shard_map/ppermute | solution.py:14
  645.6 8.0 collective-permute-done.3
  656.2 226.8 %all-reduce.8.cloned.1.call-done = f32[512,512]{1,0:T(8,128)} async-done(((f32[512,512]{1,0:T(8,128)}), f32[512,512]{1,0:T(8,128)}) %all-reduce.8.cloned.1.call-update) | async-done | bytes 1048592 | tf_op jit(solution)/shard_map/psum | solution.py:125
  883.0 3.3 gather_fusion.31
  888.3 4.5 gather_fusion.34
  892.8 2.4 gather_fusion.33
  900.7 4.5 gather_fusion.38
  905.3 2.4 gather_fusion.37
  915.0 4.5 gather_fusion.42
  919.6 2.4 gather_fusion.41
  927.2 26.8 %collective-permute-start.4 = (f32[128,256]{0,1:T(8,128)S(1)}, f32[128,256]{0,1:T(8,128)S(1)}, u32[]{:S(2)}, u32[]{:S(2)}) collective-permute-start(f32[128,256]{0,1:T(8,128)S(1)} %get-tuple-element.67), channel_id=1, source_target_pairs={{0,32},{32,64},{64,96},{96,128},{128,160},{160,192},{192,224},{224... | collective-permute-start | bytes 393224 | tf_op jit(solution)/shard_map/ppermute | solution.py:14
  955.9 8.0 collective-permute-done.5
  (166 shorter events, 75.8 us)
Async XLA Ops:
  6.5 1.0 copy-start
  6.5 244.8 %all-reduce.4.cloned.1.call-start = ((), (), s32[]{:S(2)}) async-start(), calls=%async_computation | async-start | bytes 2097152 | tf_op jit(solution)/shard_map/psum | solution.py:97
  9.5 549.0 %all-reduce.6.cloned.1.call-start = ((), (), s32[]{:S(2)}) async-start(), calls=%async_computation.1 | async-start | bytes 2097152 | tf_op jit(solution)/shard_map/psum | solution.py:125
  9.6 0.7 copy-start.19
  12.0 251.7 %copy-start.2 = (f32[512,512]{1,0:T(8,128)}, f32[512,512]{1,0:T(8,128)S(1)}, u32[]{:S(2)}) copy-start(f32[512,512]{1,0:T(8,128)S(1)} %gather_fusion.12) | copy-start | bytes 3145732
  12.0 0.7 copy-start.18
  12.7 0.7 copy-start.17
  13.4 276.9 %copy-start.14 = (s32[1024]{0:T(1024)}, s32[1024]{0:T(1024)S(1)}, u32[]{:S(2)}) copy-start(s32[1024]{0:T(1024)S(1)} %pad_clamp_fusion) | copy-start | bytes 12292
  292.9 28.7 %collective-permute-start = (f32[128,256]{0,1:T(8,128)S(1)}, f32[128,256]{0,1:T(8,128)S(1)}, u32[]{:S(2)}, u32[]{:S(2)}) collective-permute-start(f32[128,256]{0,1:T(8,128)S(1)} %get-tuple-element.75), channel_id=1, source_target_pairs={{0,32},{32,64},{64,96},{96,128},{128,160},{160,192},{192,224},{224... | collective-permute-start | bytes 393224 | tf_op jit(solution)/shard_map/ppermute | solution.py:14
  319.7 9.9 %collective-permute-start.1 = (f32[128,256]{0,1:T(8,128)S(1)}, f32[128,256]{0,1:T(8,128)S(1)}, u32[]{:S(2)}, u32[]{:S(2)}) collective-permute-start(f32[128,256]{0,1:T(8,128)S(1)} %get-tuple-element.76), channel_id=1, source_target_pairs={{32,0},{64,32},{96,64},{128,96},{160,128},{192,160},{224,192},{256... | collective-permute-start | bytes 393224 | tf_op jit(solution)/shard_map/ppermute | solution.py:14
  329.6 2.0 copy-start.13
  331.6 551.4 %all-reduce.8.cloned.1.call-start = ((), (), s32[]{:S(2)}) async-start(), calls=%async_computation.2 | async-start | bytes 2097152 | tf_op jit(solution)/shard_map/psum | solution.py:125
  580.0 1.2 copy-start.3
  597.2 1.2 copy-start.4
  608.3 2.4 copy-start.7
  608.3 2.4 copy-start.8
  612.7 0.7 copy-start.15
  616.9 28.7 %collective-permute-start.2 = (f32[128,256]{0,1:T(8,128)S(1)}, f32[128,256]{0,1:T(8,128)S(1)}, u32[]{:S(2)}, u32[]{:S(2)}) collective-permute-start(f32[128,256]{0,1:T(8,128)S(1)} %get-tuple-element.71), channel_id=1, source_target_pairs={{0,32},{32,64},{64,96},{96,128},{128,160},{160,192},{192,224},{224... | collective-permute-start | bytes 393224 | tf_op jit(solution)/shard_map/ppermute | solution.py:14
  643.7 9.9 %collective-permute-start.3 = (f32[128,256]{0,1:T(8,128)S(1)}, f32[128,256]{0,1:T(8,128)S(1)}, u32[]{:S(2)}, u32[]{:S(2)}) collective-permute-start(f32[128,256]{0,1:T(8,128)S(1)} %get-tuple-element.72), channel_id=1, source_target_pairs={{32,0},{64,32},{96,64},{128,96},{160,128},{192,160},{224,192},{256... | collective-permute-start | bytes 393224 | tf_op jit(solution)/shard_map/ppermute | solution.py:14
  653.6 0.7 copy-start.11
  905.3 2.4 copy-start.9
  905.3 2.4 copy-start.10
  919.5 2.4 copy-start.5
  919.6 2.4 copy-start.6
  923.9 0.7 copy-start.16
  924.6 1.6 copy-start.12
  927.2 28.7 %collective-permute-start.4 = (f32[128,256]{0,1:T(8,128)S(1)}, f32[128,256]{0,1:T(8,128)S(1)}, u32[]{:S(2)}, u32[]{:S(2)}) collective-permute-start(f32[128,256]{0,1:T(8,128)S(1)} %get-tuple-element.67), channel_id=1, source_target_pairs={{0,32},{32,64},{64,96},{96,128},{128,160},{160,192},{192,224},{224... | collective-permute-start | bytes 393224 | tf_op jit(solution)/shard_map/ppermute | solution.py:14
  954.0 9.9 %collective-permute-start.5 = (f32[128,256]{0,1:T(8,128)S(1)}, f32[128,256]{0,1:T(8,128)S(1)}, u32[]{:S(2)}, u32[]{:S(2)}) collective-permute-start(f32[128,256]{0,1:T(8,128)S(1)} %get-tuple-element.68), channel_id=1, source_target_pairs={{32,0},{64,32},{96,64},{128,96},{160,128},{192,160},{224,192},{256... | collective-permute-start | bytes 393224 | tf_op jit(solution)/shard_map/ppermute | solution.py:14
  963.9 1.0 copy-start.1
Sparse Core Ops, SparseCore 0:
  10.3 241.0 all-reduce.3
  331.8 226.6 all-reduce.5
  656.4 226.6 all-reduce.7
where the time goes:
time: 983 us; the launch traced here: 972 us
  waiting for transfers between devices  715 us (73%)
  local copies, waits for them, and re-layouts  136 us (14%)
  starting transfers between devices  86.1 us (9%)
  between operations  14.7 us (1%)
  other arithmetic  10.1 us (1%)
    psum x2, waiting for transfers between devices, per_device(): gram_matrix = lax.psum(local_gram(upper_block, lower_block), 'row')  454 us
    psum x1, waiting for transfers between devices, first_total(): return lax.psum(local_gram(upper_block, lower_block), 'row')  238 us
    ppermute x6, starting transfers between devices, shifted(): return lax.ppermute(x, axis, pairs)  86 us
    gather x9, local copies, waits for them, and re-layouts, angles(): diagonal = jnp.diagonal(current)  40.9 us
    gather x9, local copies, waits for them, and re-layouts, diagonalize(): current = gram_matrix[orders[0]][:, orders[0]]  24.9 us
    ppermute x6, waiting for transfers between devices, shifted(): return lax.ppermute(x, axis, pairs)  23.9 us
    gather x18, local copies, waits for them, and re-layouts, diagonalize(): current = current[relative][:, relative]  21.4 us
    gather x9, local copies, waits for them, and re-layouts, angles(): coupling = jnp.diagonal(current[:half_size, half_size:])  21.3 us
  transfers between devices with their start and end apart: 9, of which 6 were waited for; matrix products, arithmetic and copies ran while one was open for 0% of the time, Pallas kernels for 0%

commit v1 on v0

v1 whole, which is shorter than its diff:
```python
import functools

import jax
import jax.numpy as jnp
from jax import lax
from jax.experimental import pallas as pl
from jax.experimental.pallas import tpu as pltpu
from jax.sharding import Mesh, PartitionSpec as P

HALF = 256
LANES = 128
BANDS = 11
PACKED_ROWS = 24
CHUNK = 8


def lanes_of(x):
    return lax.broadcasted_iota(jnp.int32, x.shape, 1)


def roll(x, by):
    return pltpu.roll(x, by % HALF, 1)


def before(x):
    return jnp.where(lanes_of(x) == 0, x, roll(x, 1))


def after(x):
    return jnp.where(lanes_of(x) == HALF - 1, x, roll(x, -1))


def far_before(x):
    lane = lanes_of(x)
    return jnp.where(lane == 0, roll(x, -1), jnp.where(lane == 1, roll(x, 1), roll(x, 2)))


def far_after(x):
    lane = lanes_of(x)
    return jnp.where(
        lane == HALF - 1, roll(x, 1), jnp.where(lane == HALF - 2, roll(x, -1), roll(x, -2))
    )


def advance(top, bottom):
    lane = lanes_of(top)
    new_top = jnp.where(lane == 0, top, roll(jnp.where(lane == 0, bottom, top), 1))
    new_bottom = jnp.where(lane == HALF - 1, top, roll(bottom, -1))
    return new_top, new_bottom


def retreat(top, bottom):
    lane = lanes_of(top)
    rolled = roll(top, -1)
    old_top = jnp.where(lane == 0, top, jnp.where(lane == HALF - 1, bottom, rolled))
    old_bottom = jnp.where(lane == 0, rolled, roll(bottom, 1))
    return old_top, old_bottom


def turn(top, bottom, cosine, sine):
    return cosine * top - sine * bottom, sine * top + cosine * bottom


def reverse(x):
    index = LANES - 1 - lax.broadcasted_iota(jnp.int32, (x.shape[0], LANES), 1)
    flip = lambda part: jnp.take_along_axis(part, index, axis=1)
    return jnp.concatenate([flip(x[:, LANES:]), flip(x[:, :LANES])], axis=1)


def band_products(top, bottom):
    top_m, bottom_m, top_n, bottom_n = before(top), before(bottom), after(top), after(bottom)
    top_f, bottom_f = far_before(top), far_before(bottom)
    top_g, bottom_g = far_after(top), far_after(bottom)
    return (
        top * top, bottom * bottom, top * bottom,
        top_m * top_n, top_m * bottom_n, bottom_m * top_n, bottom_m * bottom_n,
        top_f * top_g, top_f * bottom_g, bottom_f * top_g, bottom_f * bottom_g,
    )


def bands_of(read, rows):
    total = None
    for start in range(0, rows, CHUNK):
        terms = band_products(*read(start))
        total = terms if total is None else [t + u for t, u in zip(total, terms)]
    sums = [jnp.sum(t, axis=0, keepdims=True) for t in total]
    blank = jnp.zeros((PACKED_ROWS - 2 * BANDS, LANES), jnp.float32)
    return jnp.concatenate(
        [s[:, :LANES] for s in sums] + [s[:, LANES:] for s in sums] + [blank], axis=0
    )


def angles(a, b, c):
    difference = b - a
    sign = jnp.where(difference >= 0, 1.0, -1.0)
    radius = jnp.sqrt(difference * difference + 4.0 * c * c + (1e-06 * (a + b)) ** 2)
    tangent = 2.0 * c * sign / (jnp.abs(difference) + radius)
    cosine = 1.0 / jnp.sqrt(1.0 + tangent * tangent)
    return cosine, tangent * cosine


def turn_diagonal(a, b, c, cosine, sine):
    cc, ss, cs = cosine * cosine, sine * sine, cosine * sine
    twice = 2.0 * cs * c
    return cc * a - twice + ss * b, ss * a + twice + cc * b, cs * (a - b) + (cc - ss) * c


def turn_block(block, left, right):
    pp, pq, qp, qq = block
    pp, qp = turn(pp, qp, *left)
    pq, qq = turn(pq, qq, *left)
    pp, pq = turn(pp, pq, *right)
    qp, qq = turn(qp, qq, *right)
    return pp, pq, qp, qq


def three_angles(packed):
    rows = [
        jnp.concatenate([packed[k : k + 1], packed[BANDS + k : BANDS + k + 1]], axis=1)
        for k in range(BANDS)
    ]
    a, b, c = rows[:3]
    lane = lanes_of(a)
    last = HALF - 1
    first = angles(a, b, c)
    a, b, c = turn_diagonal(a, b, c, *first)
    both = lambda move, pair: (move(pair[0]), move(pair[1]))
    near_pp, near_pq, near_qp, near_qq = turn_block(
        rows[3:7], both(before, first), both(after, first)
    )
    far_pp, far_pq, _, far_qq = turn_block(
        rows[7:11], both(far_before, first), both(far_after, first)
    )
    a, b = advance(a, b)
    cross = jnp.where(lane == 1, near_qq, jnp.where(lane == last, near_pp, near_pq))
    second = angles(a, b, cross)
    a, b, _ = turn_diagonal(a, b, cross, *second)
    pp = jnp.where(
        lane == 0, c, jnp.where(lane == 2, roll(near_qp, 1), jnp.where(lane == last, far_pp, roll(near_pp, 1)))
    )
    qq = jnp.where(
        lane == 0,
        far_qq,
        jnp.where(lane == last - 1, roll(near_qp, -1), jnp.where(lane == last, c, roll(near_qq, -1))),
    )
    pq = jnp.where(
        lane == 0,
        roll(near_pq, -1),
        jnp.where(
            lane == 2,
            far_qq,
            jnp.where(lane == last - 1, far_pp, jnp.where(lane == last, roll(near_pp, 1), far_pq)),
        ),
    )
    qp = jnp.where(lane == 0, near_qq, jnp.where(lane == last, near_pq, c))
    pp, pq, _, qq = turn_block((pp, pq, qp, qq), both(before, second), both(after, second))
    a, b = advance(a, b)
    cross = jnp.where(lane == 1, qq, jnp.where(lane == last, pp, pq))
    return first, second, angles(a, b, cross)


def ordered_sum(x):
    return functools.reduce(jnp.add, [x[i] for i in range(x.shape[0])])


def chosen(condition, x, y):
    return jnp.where(condition, x, y)


def wide(angle_pairs):
    return [[jnp.broadcast_to(v, (CHUNK, HALF)) for v in pair] for pair in angle_pairs]


def rotated(top, bottom, angle_pairs):
    first, second, third = angle_pairs
    top, bottom = advance(*turn(top, bottom, *first))
    top, bottom = advance(*turn(top, bottom, *second))
    top, bottom = turn(top, bottom, *third)
    return retreat(*retreat(top, bottom))


def chunks(ref):
    return [pl.ds(start, CHUNK) for start in range(0, ref.shape[0], CHUNK)]


def start_kernel(work_ref, top_ref, bottom_ref, band_ref):
    def read(start):
        row = pl.ds(start, CHUNK)
        top = work_ref[row, :HALF]
        bottom = reverse(work_ref[row, HALF:])
        top_ref[row, :] = top
        bottom_ref[row, :] = bottom
        return top, bottom

    band_ref[...] = bands_of(read, work_ref.shape[0])


def rotate_kernel(place_ref, top_ref, bottom_ref, parts_ref, kept_ref, odd_ref, even_ref):
    place = place_ref[0, 0]
    at_odd = place % 2 == 1
    angle_pairs = wide(three_angles(ordered_sum(parts_ref)))
    for row in chunks(top_ref):
        top, bottom = rotated(top_ref[row, :], bottom_ref[row, :], angle_pairs)
        right = chosen(place == 0, reverse(bottom), top)
        kept_ref[row, :] = chosen(place == 0, top, reverse(top))
        odd_ref[row, :] = chosen(at_odd, right, bottom)
        even_ref[row, :] = chosen(at_odd, bottom, right)


def arrive_kernel(count, place_ref, kept_ref, odd_ref, even_ref, top_ref, bottom_ref, band_ref):
    place = place_ref[0, 0]
    at_odd = place % 2 == 1

    def read(start):
        row = pl.ds(start, CHUNK)
        kept, odd, even = kept_ref[row, :], odd_ref[row, :], even_ref[row, :]
        top = chosen(place == 0, kept, chosen(at_odd, even, odd))
        bottom = chosen(place == count - 1, kept, chosen(at_odd, odd, even))
        top_ref[row, :] = top
        bottom_ref[row, :] = bottom
        return top, bottom

    band_ref[...] = bands_of(read, kept_ref.shape[0])


def rotate_far_kernel(count, place_ref, top_ref, bottom_ref, parts_ref, x_ref, y_ref):
    place = place_ref[0, 0]
    low = place % 4 < 2
    angle_pairs = wide(three_angles(ordered_sum(parts_ref)))
    for row in chunks(top_ref):
        top, bottom = rotated(top_ref[row, :], bottom_ref[row, :], angle_pairs)
        flip = reverse(chosen(place == 0, bottom, top))
        upper = chosen((place == 0) | (place == count - 1), flip, top)
        lower = chosen(place == 0, top, bottom)
        x_ref[row, :] = chosen(low, upper, lower)
        y_ref[row, :] = chosen(low, lower, upper)


def arrive_far_kernel(count, place_ref, x_ref, y_ref, y_in_ref, x_in_ref, *refs):
    before_refs, after_refs, band_ref = refs[:2], refs[2:4], refs[4]
    place = place_ref[0, 0]
    low = place % 4 < 2
    start_end, last_end = place == 0, place == count - 1

    def read_before(start):
        row = pl.ds(start, CHUNK)
        x, y, x_in, y_in = x_ref[row, :], y_ref[row, :], x_in_ref[row, :], y_in_ref[row, :]
        top = chosen(start_end, y, chosen(low, y_in, x_in))
        bottom = chosen(start_end, y_in, chosen(low, y, x))
        before_refs[0][row, :] = top
        before_refs[1][row, :] = bottom
        return top, bottom

    def read_after(start):
        row = pl.ds(start, CHUNK)
        x, y, x_in, y_in = x_ref[row, :], y_ref[row, :], x_in_ref[row, :], y_in_ref[row, :]
        top = chosen(low, x, chosen(last_end, y_in, y))
        bottom = chosen(low, x_in, chosen(last_end, y, y_in))
        after_refs[0][row, :] = top
        after_refs[1][row, :] = bottom
        return top, bottom

    rows = x_ref.shape[0]
    band_ref[:PACKED_ROWS, :] = bands_of(read_before, rows)
    band_ref[PACKED_ROWS:, :] = bands_of(read_after, rows)


def finish_kernel(
    count, place_ref, top_before_ref, bottom_before_ref, top_after_ref, bottom_after_ref, parts_ref, out_ref
):
    place = place_ref[0, 0]
    packed = ordered_sum(parts_ref)
    angles_before = wide(three_angles(packed[:PACKED_ROWS]))
    angles_after = wide(three_angles(packed[PACKED_ROWS:]))
    for row in chunks(out_ref):
        top, bottom = rotated(top_before_ref[row, :], bottom_before_ref[row, :], angles_before)
        out_ref[row, :HALF] = chosen(place == 1, reverse(bottom), top)
        top, bottom = rotated(top_after_ref[row, :], bottom_after_ref[row, :], angles_after)
        out_ref[row, HALF:] = chosen(place == count - 1, top, reverse(bottom))


def call(kernel, inputs, outputs, scalars=0):
    spec = pl.BlockSpec(memory_space=pltpu.VMEM)
    return pl.pallas_call(
        kernel,
        in_specs=[pl.BlockSpec(memory_space=pltpu.SMEM)] * scalars + [spec] * (len(inputs) - scalars),
        out_specs=[spec] * len(outputs),
        out_shape=[jax.ShapeDtypeStruct(shape, jnp.float32) for shape in outputs],
        compiler_params=pltpu.CompilerParams(vmem_limit_bytes=8 * 1024 * 1024),
    )(*inputs)


def from_all(x, axes):
    count = lax.axis_size(axes)
    copies = jnp.broadcast_to(x[None], (count, *x.shape))
    return lax.all_to_all(copies, axes, 0, 0, tiled=True)


def row_parts(x):
    return from_all(ordered_sum(from_all(x, ("half", "near"))), "far")


def exchange(x, edges):
    return lax.ppermute(x, "pair", edges + [(j, i) for i, j in edges])


def per_device(snapshots):
    rows = snapshots.shape[0]
    count = lax.axis_size("pair")
    place = lax.axis_index("pair").astype(jnp.int32).reshape(1, 1)
    block, packed = (rows, HALF), (PACKED_ROWS, LANES)
    line = list(range(count))
    odd_edges, even_edges = list(zip(line[1:-1:2], line[2::2])), list(zip(line[::2], line[1::2]))
    cycle = line[::2] + line[::-2]
    x_edges = list(zip(cycle[::2], cycle[1::2]))
    y_edges = list(zip(cycle[1::2], cycle[2::2] + cycle[:1]))

    top, bottom, band = call(start_kernel, [snapshots], [block, block, packed])
    kept, odd, even = call(
        rotate_kernel, [place, top, bottom, row_parts(band)], [block] * 3, 1
    )
    top, bottom, band = call(
        functools.partial(arrive_kernel, count),
        [place, kept, exchange(odd, odd_edges), exchange(even, even_edges)],
        [block, block, packed],
        1,
    )
    x, y = call(
        functools.partial(rotate_far_kernel, count),
        [place, top, bottom, row_parts(band)],
        [block] * 2,
        1,
    )
    y_in = exchange(y, y_edges)
    x_in = exchange(x, x_edges)
    *blocks, band = call(
        functools.partial(arrive_far_kernel, count),
        [place, x, y, y_in, x_in],
        [block] * 4 + [(2 * PACKED_ROWS, LANES)],
        1,
    )
    (out,) = call(
        functools.partial(finish_kernel, count),
        [place, *blocks, row_parts(band)],
        [(rows, 2 * HALF)],
        1,
    )
    return out


def solution(mesh):
    pairs, rows = mesh.devices.shape
    fine = Mesh(mesh.devices.reshape(pairs, 2, rows // 4, 2), ("pair", "half", "far", "near"))
    spec = P(("half", "far", "near"), "pair")
    return jax.shard_map(
        per_device, mesh=fine, in_specs=(spec,), out_specs=spec, check_vma=False
    )
```

time: 983 us -> 118 us (0.12)
  the two profiles are of different devices: /device:TPU:25 before, /device:TPU:4 now
where the time goes in v1:
time: 118 us; the launch traced here: 117 us
  blocking collectives  57.9 us (49%)
  waiting for transfers between devices  25.3 us (21%)
  starting transfers between devices  24.7 us (21%)
  Pallas kernels  7.71 us (7%)
  local copies, waits for them, and re-layouts  1.64 us (1%)
    all_to_all x5, blocking collectives, from_all(): return lax.all_to_all(copies, axes, 0, 0, tiled=True)  57.9 us
    all_to_all x1, starting transfers between devices, from_all(): return lax.all_to_all(copies, axes, 0, 0, tiled=True)  14.2 us
    all_to_all x1, waiting for transfers between devices, from_all(): return lax.all_to_all(copies, axes, 0, 0, tiled=True)  13.5 us
    ppermute x4, waiting for transfers between devices, exchange(): return lax.ppermute(x, 'pair', edges + [(j, i) for i, j in edges])  11.7 us
    ppermute x4, starting transfers between devices, exchange(): return lax.ppermute(x, 'pair', edges + [(j, i) for i, j in edges])  10.5 us
    pallas_call x6, Pallas kernels, call(): pl.pallas_call(kernel, in_specs=[pl.BlockSpec(memory_space=pltpu.SMEM)] *...  7.71 us
  transfers between devices with their start and end apart: 5, of which 4 were waited for; matrix products, arithmetic and copies ran while one was open for 0% of the time, Pallas kernels for 0%

profile of v1, /device:TPU:4, one launch (start us, length us, event | category | flops | bytes accessed | tf_op | source)
XLA Modules:
  0.0 117.3 jit_solution(2017571336161209008)
XLA Ops:
  0.0 0.0 copy-start
  0.0 0.9 copy-done
  1.0 1.0 shard_map.17
  2.0 8.4 %all_to_all.30 = f32[4,24,128]{2,1,0:T(8,128)S(1)} all-to-all(f32[4,24,128]{2,1,0:T(8,128)S(1)} %broadcast_in_dim.18), channel_id=1, replica_groups=mesh['pair'=16,'half'=2,'far'=8,'near'=2] {'half','near'}, dimensions={0} | all-to-all | bytes 98304 | tf_op jit(solution)/shard_map/all_to_all | solution.py:296
  10.4 0.7 broadcast_in_dim.20
  11.0 14.2 %all-to-all-start.1 = ((f32[8,24,128]{2,1,0:T(8,128)}), f32[8,24,128]{2,1,0:T(8,128)S(1)}, u32[]{:S(2)}, u32[]{:S(2)}) async-start(f32[8,24,128]{2,1,0:T(8,128)} %broadcast_in_dim.20), calls=%async_computation.1 | async-start | bytes 196608 | tf_op jit(solution)/shard_map/all_to_all | solution.py:296
  25.2 13.5 %all-to-all-done.1.parts_ref = f32[8,24,128]{2,1,0:T(8,128)S(1)} async-done(((f32[8,24,128]{2,1,0:T(8,128)}), f32[8,24,128]{2,1,0:T(8,128)S(1)}, u32[]{:S(2)}, u32[]{:S(2)}) %all-to-all-start.1) | async-done | bytes 98336 | tf_op jit(solution)/shard_map/all_to_all | solution.py:296
  38.8 0.8 shard_map.18
  39.6 2.0 %collective-permute-start = (f32[128,256]{1,0:T(8,128)S(1)}, f32[128,256]{1,0:T(8,128)S(1)}, u32[]{:S(2)}, u32[]{:S(2)}) collective-permute-start(f32[128,256]{1,0:T(8,128)S(1)} %get-tuple-element.25), channel_id=1, source_target_pairs={{32,64},{96,128},{160,192},{224,256},{288,320},{352,384},{416,448}... | collective-permute-start | bytes 393224 | tf_op jit(solution)/shard_map/ppermute | solution.py:304
  41.6 3.5 %collective-permute-start.1 = (f32[128,256]{1,0:T(8,128)S(1)}, f32[128,256]{1,0:T(8,128)S(1)}, u32[]{:S(2)}, u32[]{:S(2)}) collective-permute-start(f32[128,256]{1,0:T(8,128)S(1)} %get-tuple-element.26), channel_id=1, source_target_pairs={{0,32},{64,96},{128,160},{192,224},{256,288},{320,352},{384,416},{... | collective-permute-start | bytes 393224 | tf_op jit(solution)/shard_map/ppermute | solution.py:304
  45.1 4.4 %collective-permute-done.odd_ref = f32[128,256]{1,0:T(8,128)S(1)} collective-permute-done((f32[128,256]{1,0:T(8,128)S(1)}, f32[128,256]{1,0:T(8,128)S(1)}, u32[]{:S(2)}, u32[]{:S(2)}) %collective-permute-start) | collective-permute-done | bytes 131104 | tf_op jit(solution)/shard_map/ppermute | solution.py:304
  49.5 0.0 collective-permute-done.1.even_ref
  49.5 0.4 shard_map.19
  49.8 7.3 %all_to_all.31 = f32[4,24,128]{2,1,0:T(8,128)S(1)} all-to-all(f32[4,24,128]{2,1,0:T(8,128)S(1)} %broadcast_in_dim.21), channel_id=1, replica_groups=mesh['pair'=16,'half'=2,'far'=8,'near'=2] {'half','near'}, dimensions={0} | all-to-all | bytes 98304 | tf_op jit(solution)/shard_map/all_to_all | solution.py:296
  57.2 16.1 %all_to_all.32.parts_ref = f32[8,24,128]{2,1,0:T(8,128)S(1)} all-to-all(f32[8,24,128]{2,1,0:T(8,128)S(1)} %broadcast_in_dim.23), channel_id=1, replica_groups=mesh['pair'=16,'half'=2,'far'=8,'near'=2] {'far'}, dimensions={0} | all-to-all | bytes 196608 | tf_op jit(solution)/shard_map/all_to_all | solution.py:296
  73.3 0.7 shard_map.20
  74.0 1.9 %collective-permute-start.3 = (f32[128,256]{1,0:T(8,128)S(1)}, f32[128,256]{1,0:T(8,128)S(1)}, u32[]{:S(2)}, u32[]{:S(2)}) collective-permute-start(f32[128,256]{1,0:T(8,128)S(1)} %get-tuple-element.30.x_ref), channel_id=1, source_target_pairs={{0,64},{128,192},{256,320},{384,448},{480,416},{352,288},{224,160}... | collective-permute-start | bytes 393224 | tf_op jit(solution)/shard_map/ppermute | solution.py:304
  75.9 3.1 %collective-permute-start.2 = (f32[128,256]{1,0:T(8,128)S(1)}, f32[128,256]{1,0:T(8,128)S(1)}, u32[]{:S(2)}, u32[]{:S(2)}) collective-permute-start(f32[128,256]{1,0:T(8,128)S(1)} %get-tuple-element.31.y_ref), channel_id=1, source_target_pairs={{64,128},{192,256},{320,384},{448,480},{416,352},{288,224},{160,96... | collective-permute-start | bytes 393224 | tf_op jit(solution)/shard_map/ppermute | solution.py:304
  79.1 1.8 %collective-permute-done.3.x_in_ref = f32[128,256]{1,0:T(8,128)S(1)} collective-permute-done((f32[128,256]{1,0:T(8,128)S(1)}, f32[128,256]{1,0:T(8,128)S(1)}, u32[]{:S(2)}, u32[]{:S(2)}) %collective-permute-start.3) | collective-permute-done | bytes 131104 | tf_op jit(solution)/shard_map/ppermute | solution.py:304
  80.9 5.5 %collective-permute-done.2.y_in_ref = f32[128,256]{1,0:T(8,128)S(1)} collective-permute-done((f32[128,256]{1,0:T(8,128)S(1)}, f32[128,256]{1,0:T(8,128)S(1)}, u32[]{:S(2)}, u32[]{:S(2)}) %collective-permute-start.2) | collective-permute-done | bytes 131104 | tf_op jit(solution)/shard_map/ppermute | solution.py:304
  86.4 0.7 shard_map.21
  87.1 7.3 %all_to_all.33 = f32[4,48,128]{2,1,0:T(8,128)S(1)} all-to-all(f32[4,48,128]{2,1,0:T(8,128)S(1)} %broadcast_in_dim.48), channel_id=1, replica_groups=mesh['pair'=16,'half'=2,'far'=8,'near'=2] {'half','near'}, dimensions={0} | all-to-all | bytes 196608 | tf_op jit(solution)/shard_map/all_to_all | solution.py:296
  94.4 18.7 %all_to_all.34.parts_ref = f32[8,48,128]{2,1,0:T(8,128)S(1)} all-to-all(f32[8,48,128]{2,1,0:T(8,128)S(1)} %broadcast_in_dim.50), channel_id=1, replica_groups=mesh['pair'=16,'half'=2,'far'=8,'near'=2] {'far'}, dimensions={0} | all-to-all | bytes 393216 | tf_op jit(solution)/shard_map/all_to_all | solution.py:296
  113.2 4.2 %shard_map.22 = f32[128,512]{1,0:T(8,128)} custom-call(s32[1,1]{1,0:T(1,128)} %bitcast.place_ref, f32[128,256]{1,0:T(8,128)S(1)} %get-tuple-element.32.top_before_ref, f32[128,256]{1,0:T(8,128)S(1)} %get-tuple-element.33.bottom_before_ref, f32[128,256]{1,0:T(8,128)S(1)} %get-tuple-element.34.top_after_ref, ...), custom_call_target="tpu_custom_call" | custom-call | tf_op jit(solution)/shard_map/pallas_call | solution.py:284
  (8 shorter events, 0.1 us)
Async XLA Ops:
  0.0 0.9 copy-start
  11.0 27.7 %all-to-all-start.1 = ((f32[8,24,128]{2,1,0:T(8,128)}), f32[8,24,128]{2,1,0:T(8,128)S(1)}, u32[]{:S(2)}, u32[]{:S(2)}) async-start(f32[8,24,128]{2,1,0:T(8,128)} %broadcast_in_dim.20), calls=%async_computation.1 | async-start | bytes 196608 | tf_op jit(solution)/shard_map/all_to_all | solution.py:296
  39.6 9.9 %collective-permute-start = (f32[128,256]{1,0:T(8,128)S(1)}, f32[128,256]{1,0:T(8,128)S(1)}, u32[]{:S(2)}, u32[]{:S(2)}) collective-permute-start(f32[128,256]{1,0:T(8,128)S(1)} %get-tuple-element.25), channel_id=1, source_target_pairs={{32,64},{96,128},{160,192},{224,256},{288,320},{352,384},{416,448}... | collective-permute-start | bytes 393224 | tf_op jit(solution)/shard_map/ppermute | solution.py:304
  41.6 7.9 %collective-permute-start.1 = (f32[128,256]{1,0:T(8,128)S(1)}, f32[128,256]{1,0:T(8,128)S(1)}, u32[]{:S(2)}, u32[]{:S(2)}) collective-permute-start(f32[128,256]{1,0:T(8,128)S(1)} %get-tuple-element.26), channel_id=1, source_target_pairs={{0,32},{64,96},{128,160},{192,224},{256,288},{320,352},{384,416},{... | collective-permute-start | bytes 393224 | tf_op jit(solution)/shard_map/ppermute | solution.py:304
  74.0 6.9 %collective-permute-start.3 = (f32[128,256]{1,0:T(8,128)S(1)}, f32[128,256]{1,0:T(8,128)S(1)}, u32[]{:S(2)}, u32[]{:S(2)}) collective-permute-start(f32[128,256]{1,0:T(8,128)S(1)} %get-tuple-element.30.x_ref), channel_id=1, source_target_pairs={{0,64},{128,192},{256,320},{384,448},{480,416},{352,288},{224,160}... | collective-permute-start | bytes 393224 | tf_op jit(solution)/shard_map/ppermute | solution.py:304
  75.9 10.5 %collective-permute-start.2 = (f32[128,256]{1,0:T(8,128)S(1)}, f32[128,256]{1,0:T(8,128)S(1)}, u32[]{:S(2)}, u32[]{:S(2)}) collective-permute-start(f32[128,256]{1,0:T(8,128)S(1)} %get-tuple-element.31.y_ref), channel_id=1, source_target_pairs={{64,128},{192,256},{320,384},{448,480},{416,352},{288,224},{160,96... | collective-permute-start | bytes 393224 | tf_op jit(solution)/shard_map/ppermute | solution.py:304

commit v2 on v1

v2 whole, which is shorter than its diff:
```python
import functools

import jax
import jax.numpy as jnp
from jax import lax
from jax.experimental import pallas as pl
from jax.experimental.pallas import tpu as pltpu
from jax.sharding import Mesh, PartitionSpec as P

HALF = 256
LANES = 128
BANDS = 11
PACKED_ROWS = 24
CHUNK = 8


def lanes_of(x):
    return lax.broadcasted_iota(jnp.int32, x.shape, 1)


def roll(x, by):
    return pltpu.roll(x, by % HALF, 1)


def halves(x):
    return x[:, :LANES], x[:, LANES:]


def reverse(x):
    left, right = halves(x)
    return jnp.concatenate([right, left], axis=1)


def split(top, bottom):
    (top_left, top_right), (bottom_left, bottom_right) = halves(top), halves(bottom)
    ahead = jnp.concatenate([top_left, bottom_right], axis=1)
    back = jnp.concatenate([bottom_left, top_right], axis=1)
    return ahead, back


def pick(x, index):
    return jnp.take_along_axis(x, index, axis=1)


def to_cycle(x):
    left, right = halves(x)
    lane = lanes_of(left)
    up, down = 2 * lane % LANES, (2 * LANES - 1 - 2 * lane) % LANES
    first = lane < LANES // 2
    return jnp.concatenate(
        [
            jnp.where(first, pick(left, up), pick(right, up)),
            jnp.where(first, pick(right, down), pick(left, down)),
        ],
        axis=1,
    )


def from_cycle(x):
    left, right = halves(x)
    lane = lanes_of(left)
    half = lane // 2
    even = lane % 2 == 0
    low = jnp.where(even, pick(left, half), pick(right, LANES - 1 - half))
    high = jnp.where(even, pick(left, LANES // 2 + half), pick(right, LANES // 2 - 1 - half))
    return jnp.concatenate([low, high], axis=1)


def turn(ahead, back, matrix):
    m00, m01, m10, m11 = matrix
    return m00 * ahead + m01 * back, m10 * ahead + m11 * back


def swap_at(lane, ahead, back):
    here = lanes_of(ahead) == lane
    return jnp.where(here, back, ahead), jnp.where(here, ahead, back)


def band_products(top, bottom):
    f, b = split(top, bottom)
    f1, b1, f2, b2 = roll(f, -1), roll(b, -1), roll(f, -2), roll(b, -2)
    return f * f, b * b, f * b, f * f1, f * b1, b * f1, b * b1, f * f2, f * b2, b * f2, b * b2


def bands_of(read, rows):
    total = None
    for start in range(0, rows, CHUNK):
        terms = band_products(*read(start))
        total = terms if total is None else [t + u for t, u in zip(total, terms)]
    return [jnp.sum(t, axis=0, keepdims=True) for t in total]


def pack(*pair_bands):
    left = [bands[k][:, :LANES] for k in range(BANDS) for bands in pair_bands]
    right = [bands[k][:, LANES:] for k in range(BANDS) for bands in pair_bands]
    blank = jnp.zeros((len(pair_bands) * (PACKED_ROWS - 2 * BANDS), LANES), jnp.float32)
    return jnp.concatenate(left + right + [blank], axis=0)


def unpack(packed):
    count = packed.shape[0] // PACKED_ROWS
    rows = [packed[k * count : (k + 1) * count] for k in range(2 * BANDS)]
    return [jnp.concatenate([rows[k], rows[BANDS + k]], axis=1) for k in range(BANDS)]


def matrix_of(ff, bb, fb, upper_ahead, swapped_lane):
    a, b, c = jnp.where(upper_ahead, ff, bb), jnp.where(upper_ahead, bb, ff), fb
    difference = b - a
    sign = jnp.where(difference >= 0, 1.0, -1.0)
    radius = jnp.sqrt(difference * difference + 4.0 * c * c + (1e-06 * (a + b)) ** 2)
    tangent = 2.0 * c * sign / (jnp.abs(difference) + radius)
    cosine = 1.0 / jnp.sqrt(1.0 + tangent * tangent)
    sine = tangent * cosine
    sine = jnp.where(upper_ahead, sine, -sine)
    if swapped_lane is None:
        return cosine, -sine, sine, cosine
    here = lanes_of(ff) == swapped_lane
    rows = jnp.where(here, sine, cosine), jnp.where(here, cosine, sine)
    return rows[0], jnp.where(here, cosine, -sine), rows[1], jnp.where(here, -sine, cosine)


def turn_diagonal(ff, bb, fb, matrix):
    m00, m01, m10, m11 = matrix
    return (
        m00 * m00 * ff + 2.0 * m00 * m01 * fb + m01 * m01 * bb,
        m10 * m10 * ff + 2.0 * m10 * m11 * fb + m11 * m11 * bb,
        m00 * m10 * ff + (m00 * m11 + m01 * m10) * fb + m01 * m11 * bb,
    )


def turn_block(block, left, right):
    ff, fb, bf, bb = block
    ff, bf = turn(ff, bf, left)
    fb, bb = turn(fb, bb, left)
    ff, fb = turn(ff, fb, right)
    bf, bb = turn(bf, bb, right)
    return ff, fb, bf, bb


def shifted(matrix, by):
    return [roll(m, -by) for m in matrix]


def three_matrices(packed):
    rows = unpack(packed)
    lane = lanes_of(rows[0])
    left = lane < LANES
    first = matrix_of(*rows[:3], left, 0)
    ff, bb, fb = turn_diagonal(*rows[:3], first)
    near_ff, near_fb, _, near_bb = turn_block(rows[3:7], first, shifted(first, 1))
    _, far_fb, _, _ = turn_block(rows[7:11], first, shifted(first, 2))
    diagonal = ff, roll(bb, -1), near_fb
    second = matrix_of(*diagonal, left, HALF - 1)
    block = near_ff, far_fb, roll(fb, -1), roll(near_bb, -1)
    ff, bb, _ = turn_diagonal(*diagonal, second)
    _, cross, _, _ = turn_block(block, second, shifted(second, 1))
    upper_ahead = (lane < LANES - 1) | (lane == HALF - 1)
    return first, second, matrix_of(ff, roll(bb, -1), cross, upper_ahead, None)


def ordered_sum(x):
    return functools.reduce(jnp.add, [x[i] for i in range(x.shape[0])])


def chosen(condition, x, y):
    return jnp.where(condition, x, y)


def wide(matrices, index=0):
    row = slice(index, index + 1)
    return [[jnp.broadcast_to(v[row], (CHUNK, HALF)) for v in matrix] for matrix in matrices]


def rotated(top, bottom, matrices):
    first, second, third = matrices
    ahead, back = turn(*split(top, bottom), first)
    ahead, back = turn(ahead, roll(back, -1), second)
    ahead, back = turn(ahead, roll(back, -1), third)
    ahead, back = swap_at(HALF - 1, ahead, roll(back, 1))
    return split(*swap_at(0, ahead, roll(back, 1)))


def chunks(ref):
    return [pl.ds(start, CHUNK) for start in range(0, ref.shape[0], CHUNK)]


def start_kernel(work_ref, top_ref, bottom_ref, band_ref):
    def read(start):
        row = pl.ds(start, CHUNK)
        top = to_cycle(work_ref[row, :HALF])
        bottom = reverse(to_cycle(work_ref[row, HALF:]))
        top_ref[row, :] = top
        bottom_ref[row, :] = bottom
        return top, bottom

    band_ref[...] = pack(bands_of(read, work_ref.shape[0]))


def rotate_kernel(place_ref, top_ref, bottom_ref, parts_ref, kept_ref, odd_ref, even_ref):
    place = place_ref[0, 0]
    at_odd = place % 2 == 1
    matrices = wide(three_matrices(ordered_sum(parts_ref)))
    for row in chunks(top_ref):
        top, bottom = rotated(top_ref[row, :], bottom_ref[row, :], matrices)
        right = chosen(place == 0, reverse(bottom), top)
        kept_ref[row, :] = chosen(place == 0, top, reverse(top))
        odd_ref[row, :] = chosen(at_odd, right, bottom)
        even_ref[row, :] = chosen(at_odd, bottom, right)


def arrive_kernel(count, place_ref, kept_ref, odd_ref, even_ref, top_ref, bottom_ref, band_ref):
    place = place_ref[0, 0]
    at_odd = place % 2 == 1

    def read(start):
        row = pl.ds(start, CHUNK)
        kept, odd, even = kept_ref[row, :], odd_ref[row, :], even_ref[row, :]
        top = chosen(place == 0, kept, chosen(at_odd, even, odd))
        bottom = chosen(place == count - 1, kept, chosen(at_odd, odd, even))
        top_ref[row, :] = top
        bottom_ref[row, :] = bottom
        return top, bottom

    band_ref[...] = pack(bands_of(read, kept_ref.shape[0]))


def rotate_far_kernel(count, place_ref, top_ref, bottom_ref, parts_ref, y_ref, x_ref):
    place = place_ref[0, 0]
    low = place % 4 < 2
    matrices = wide(three_matrices(ordered_sum(parts_ref)))
    for row in chunks(top_ref):
        top, bottom = rotated(top_ref[row, :], bottom_ref[row, :], matrices)
        flip = reverse(chosen(place == 0, bottom, top))
        upper = chosen((place == 0) | (place == count - 1), flip, top)
        lower = chosen(place == 0, top, bottom)
        x_ref[row, :] = chosen(low, upper, lower)
        y_ref[row, :] = chosen(low, lower, upper)


def arrive_far_kernel(count, place_ref, y_ref, x_ref, y_in_ref, x_in_ref, *refs):
    before_refs, after_refs, band_ref = refs[:2], refs[2:4], refs[4]
    place = place_ref[0, 0]
    low = place % 4 < 2
    start_end, last_end = place == 0, place == count - 1

    def read_before(start):
        row = pl.ds(start, CHUNK)
        x, y, x_in, y_in = x_ref[row, :], y_ref[row, :], x_in_ref[row, :], y_in_ref[row, :]
        top = chosen(start_end, y, chosen(low, y_in, x_in))
        bottom = chosen(start_end, y_in, chosen(low, y, x))
        before_refs[0][row, :] = top
        before_refs[1][row, :] = bottom
        return top, bottom

    def read_after(start):
        row = pl.ds(start, CHUNK)
        x, y, x_in, y_in = x_ref[row, :], y_ref[row, :], x_in_ref[row, :], y_in_ref[row, :]
        top = chosen(low, x, chosen(last_end, y_in, y))
        bottom = chosen(low, x_in, chosen(last_end, y, y_in))
        after_refs[0][row, :] = top
        after_refs[1][row, :] = bottom
        return top, bottom

    rows = x_ref.shape[0]
    band_ref[...] = pack(bands_of(read_before, rows), bands_of(read_after, rows))


def finish_kernel(
    count, place_ref, top_before_ref, bottom_before_ref, top_after_ref, bottom_after_ref, parts_ref, out_ref
):
    place = place_ref[0, 0]
    both = three_matrices(ordered_sum(parts_ref))
    matrices_before, matrices_after = wide(both, 0), wide(both, 1)
    for row in chunks(out_ref):
        top, bottom = rotated(top_before_ref[row, :], bottom_before_ref[row, :], matrices_before)
        out_ref[row, :HALF] = from_cycle(chosen(place == 1, reverse(bottom), top))
        top, bottom = rotated(top_after_ref[row, :], bottom_after_ref[row, :], matrices_after)
        out_ref[row, HALF:] = from_cycle(chosen(place == count - 1, top, reverse(bottom)))


def call(kernel, inputs, outputs, scalars=0):
    spec = pl.BlockSpec(memory_space=pltpu.VMEM)
    return pl.pallas_call(
        kernel,
        in_specs=[pl.BlockSpec(memory_space=pltpu.SMEM)] * scalars + [spec] * (len(inputs) - scalars),
        out_specs=[spec] * len(outputs),
        out_shape=[jax.ShapeDtypeStruct(shape, jnp.float32) for shape in outputs],
        compiler_params=pltpu.CompilerParams(vmem_limit_bytes=8 * 1024 * 1024),
    )(*inputs)


def from_all(x, axes):
    count = lax.axis_size(axes)
    copies = jnp.broadcast_to(x[None], (count, *x.shape))
    return lax.all_to_all(copies, axes, 0, 0, tiled=True)


def row_parts(x):
    return from_all(ordered_sum(from_all(x, ("half", "near"))), "far")


def exchange(x, edges):
    return lax.ppermute(x, "pair", edges + [(j, i) for i, j in edges])


def per_device(snapshots):
    rows = snapshots.shape[0]
    count = lax.axis_size("pair")
    place = lax.axis_index("pair").astype(jnp.int32).reshape(1, 1)
    block, packed = (rows, HALF), (PACKED_ROWS, LANES)
    line = list(range(count))
    odd_edges, even_edges = list(zip(line[1:-1:2], line[2::2])), list(zip(line[::2], line[1::2]))
    cycle = line[::2] + line[::-2]
    x_edges = list(zip(cycle[::2], cycle[1::2]))
    y_edges = list(zip(cycle[1::2], cycle[2::2] + cycle[:1]))

    top, bottom, band = call(start_kernel, [snapshots], [block, block, packed])
    kept, odd, even = call(
        rotate_kernel, [place, top, bottom, row_parts(band)], [block] * 3, 1
    )
    top, bottom, band = call(
        functools.partial(arrive_kernel, count),
        [place, kept, exchange(odd, odd_edges), exchange(even, even_edges)],
        [block, block, packed],
        1,
    )
    y, x = call(
        functools.partial(rotate_far_kernel, count),
        [place, top, bottom, row_parts(band)],
        [block] * 2,
        1,
    )
    y_in = exchange(y, y_edges)
    x_in = exchange(x, x_edges)
    *blocks, band = call(
        functools.partial(arrive_far_kernel, count),
        [place, y, x, y_in, x_in],
        [block] * 4 + [(2 * PACKED_ROWS, LANES)],
        1,
    )
    (out,) = call(
        functools.partial(finish_kernel, count),
        [place, *blocks, row_parts(band)],
        [(rows, 2 * HALF)],
        1,
    )
    return out


def solution(mesh):
    pairs, rows = mesh.devices.shape
    fine = Mesh(mesh.devices.reshape(pairs, 2, rows // 4, 2), ("pair", "half", "far", "near"))
    spec = P(("half", "far", "near"), "pair")
    return jax.shard_map(
        per_device, mesh=fine, in_specs=(spec,), out_specs=spec, check_vma=False
    )
```

time: 118 us -> 114 us (0.966)
  the two profiles are of different devices: /device:TPU:4 before, /device:TPU:16 now
where the time goes in v2:
time: 114 us
  blocking collectives  59.9 us (53%)
  starting transfers between devices  30 us (26%)
  waiting for transfers between devices  17.5 us (15%)
  Pallas kernels  4.46 us (4%)
  local copies, waits for them, and re-layouts  1.64 us (1%)
    all_to_all x5, blocking collectives, from_all(): return lax.all_to_all(copies, axes, 0, 0, tiled=True)  59.9 us
    ppermute x4, starting transfers between devices, exchange(): return lax.ppermute(x, 'pair', edges + [(j, i) for i, j in edges])  15.9 us
    all_to_all x1, starting transfers between devices, from_all(): return lax.all_to_all(copies, axes, 0, 0, tiled=True)  14.2 us
    all_to_all x1, waiting for transfers between devices, from_all(): return lax.all_to_all(copies, axes, 0, 0, tiled=True)  13.5 us
    pallas_call x6, Pallas kernels, call(): pl.pallas_call(kernel, in_specs=[pl.BlockSpec(memory_space=pltpu.SMEM)] *...  4.46 us
    ppermute x4, waiting for transfers between devices, exchange(): return lax.ppermute(x, 'pair', edges + [(j, i) for i, j in edges])  3.98 us
  transfers between devices with their start and end apart: 5, of which 3 were waited for; matrix products, arithmetic and copies ran while one was open for 0% of the time, Pallas kernels for 0%

profile of v2, /device:TPU:16, one launch (start us, length us, event | category | flops | bytes accessed | tf_op | source)
XLA Modules:
  0.0 113.7 jit_solution(652005630244790889)
XLA Ops:
  0.0 0.0 copy-start
  0.0 0.9 copy-done
  1.0 1.1 shard_map.17
  2.1 8.7 %all_to_all.30 = f32[4,24,128]{2,1,0:T(8,128)S(1)} all-to-all(f32[4,24,128]{2,1,0:T(8,128)S(1)} %broadcast_in_dim.18), channel_id=1, replica_groups=mesh['pair'=16,'half'=2,'far'=8,'near'=2] {'half','near'}, dimensions={0} | all-to-all | bytes 98304 | tf_op jit(solution)/shard_map/all_to_all | solution.py:295
  10.8 0.7 broadcast_in_dim.20
  11.5 14.2 %all-to-all-start.1 = ((f32[8,24,128]{2,1,0:T(8,128)}), f32[8,24,128]{2,1,0:T(8,128)S(1)}, u32[]{:S(2)}, u32[]{:S(2)}) async-start(f32[8,24,128]{2,1,0:T(8,128)} %broadcast_in_dim.20), calls=%async_computation.1 | async-start | bytes 196608 | tf_op jit(solution)/shard_map/all_to_all | solution.py:295
  25.7 13.5 %all-to-all-done.1.parts_ref = f32[8,24,128]{2,1,0:T(8,128)S(1)} async-done(((f32[8,24,128]{2,1,0:T(8,128)}), f32[8,24,128]{2,1,0:T(8,128)S(1)}, u32[]{:S(2)}, u32[]{:S(2)}) %all-to-all-start.1) | async-done | bytes 98336 | tf_op jit(solution)/shard_map/all_to_all | solution.py:295
  39.2 0.5 shard_map.18
  39.7 1.9 %collective-permute-start = (f32[128,256]{1,0:T(8,128)S(1)}, f32[128,256]{1,0:T(8,128)S(1)}, u32[]{:S(2)}, u32[]{:S(2)}) collective-permute-start(f32[128,256]{1,0:T(8,128)S(1)} %get-tuple-element.25), channel_id=1, source_target_pairs={{32,64},{96,128},{160,192},{224,256},{288,320},{352,384},{416,448}... | collective-permute-start | bytes 393224 | tf_op jit(solution)/shard_map/ppermute | solution.py:303
  41.6 3.3 %collective-permute-start.1 = (f32[128,256]{1,0:T(8,128)S(1)}, f32[128,256]{1,0:T(8,128)S(1)}, u32[]{:S(2)}, u32[]{:S(2)}) collective-permute-start(f32[128,256]{1,0:T(8,128)S(1)} %get-tuple-element.26), channel_id=1, source_target_pairs={{0,32},{64,96},{128,160},{192,224},{256,288},{320,352},{384,416},{... | collective-permute-start | bytes 393224 | tf_op jit(solution)/shard_map/ppermute | solution.py:303
  44.9 1.1 collective-permute-done.odd_ref
  46.0 0.0 collective-permute-done.1.even_ref
  46.0 0.2 shard_map.19
  46.2 7.2 %all_to_all.31 = f32[4,24,128]{2,1,0:T(8,128)S(1)} all-to-all(f32[4,24,128]{2,1,0:T(8,128)S(1)} %broadcast_in_dim.21), channel_id=1, replica_groups=mesh['pair'=16,'half'=2,'far'=8,'near'=2] {'half','near'}, dimensions={0} | all-to-all | bytes 98304 | tf_op jit(solution)/shard_map/all_to_all | solution.py:295
  53.4 16.7 %all_to_all.32.parts_ref = f32[8,24,128]{2,1,0:T(8,128)S(1)} all-to-all(f32[8,24,128]{2,1,0:T(8,128)S(1)} %broadcast_in_dim.23), channel_id=1, replica_groups=mesh['pair'=16,'half'=2,'far'=8,'near'=2] {'far'}, dimensions={0} | all-to-all | bytes 196608 | tf_op jit(solution)/shard_map/all_to_all | solution.py:295
  70.1 0.5 shard_map.20
  70.6 2.7 %collective-permute-start.2 = (f32[128,256]{1,0:T(8,128)S(1)}, f32[128,256]{1,0:T(8,128)S(1)}, u32[]{:S(2)}, u32[]{:S(2)}) collective-permute-start(f32[128,256]{1,0:T(8,128)S(1)} %get-tuple-element.30.y_ref), channel_id=1, source_target_pairs={{64,128},{192,256},{320,384},{448,480},{416,352},{288,224},{160,96... | collective-permute-start | bytes 393224 | tf_op jit(solution)/shard_map/ppermute | solution.py:303
  73.3 8.0 %collective-permute-start.3 = (f32[128,256]{1,0:T(8,128)S(1)}, f32[128,256]{1,0:T(8,128)S(1)}, u32[]{:S(2)}, u32[]{:S(2)}) collective-permute-start(f32[128,256]{1,0:T(8,128)S(1)} %get-tuple-element.31.x_ref), channel_id=1, source_target_pairs={{0,64},{128,192},{256,320},{384,448},{480,416},{352,288},{224,160}... | collective-permute-start | bytes 393224 | tf_op jit(solution)/shard_map/ppermute | solution.py:303
  81.3 0.0 collective-permute-done.2.y_in_ref
  81.3 2.9 %collective-permute-done.3.x_in_ref = f32[128,256]{1,0:T(8,128)S(1)} collective-permute-done((f32[128,256]{1,0:T(8,128)S(1)}, f32[128,256]{1,0:T(8,128)S(1)}, u32[]{:S(2)}, u32[]{:S(2)}) %collective-permute-start.3) | collective-permute-done | bytes 131104 | tf_op jit(solution)/shard_map/ppermute | solution.py:303
  84.2 0.4 shard_map.21
  84.6 8.0 %all_to_all.33 = f32[4,48,128]{2,1,0:T(8,128)S(1)} all-to-all(f32[4,48,128]{2,1,0:T(8,128)S(1)} %broadcast_in_dim.48), channel_id=1, replica_groups=mesh['pair'=16,'half'=2,'far'=8,'near'=2] {'half','near'}, dimensions={0} | all-to-all | bytes 196608 | tf_op jit(solution)/shard_map/all_to_all | solution.py:295
  92.7 19.2 %all_to_all.34.parts_ref = f32[8,48,128]{2,1,0:T(8,128)S(1)} all-to-all(f32[8,48,128]{2,1,0:T(8,128)S(1)} %broadcast_in_dim.50), channel_id=1, replica_groups=mesh['pair'=16,'half'=2,'far'=8,'near'=2] {'far'}, dimensions={0} | all-to-all | bytes 393216 | tf_op jit(solution)/shard_map/all_to_all | solution.py:295
  111.9 1.7 %shard_map.22 = f32[128,512]{1,0:T(8,128)} custom-call(s32[1,1]{1,0:T(1,128)} %bitcast.place_ref, f32[128,256]{1,0:T(8,128)S(1)} %get-tuple-element.32.top_before_ref, f32[128,256]{1,0:T(8,128)S(1)} %get-tuple-element.33.bottom_before_ref, f32[128,256]{1,0:T(8,128)S(1)} %get-tuple-element.34.top_after_ref, ...), custom_call_target="tpu_custom_call" | custom-call | tf_op jit(solution)/shard_map/pallas_call | solution.py:283
  (8 shorter events, 0.1 us)
Async XLA Ops:
  0.0 0.9 copy-start
  11.5 27.7 %all-to-all-start.1 = ((f32[8,24,128]{2,1,0:T(8,128)}), f32[8,24,128]{2,1,0:T(8,128)S(1)}, u32[]{:S(2)}, u32[]{:S(2)}) async-start(f32[8,24,128]{2,1,0:T(8,128)} %broadcast_in_dim.20), calls=%async_computation.1 | async-start | bytes 196608 | tf_op jit(solution)/shard_map/all_to_all | solution.py:295
  39.7 6.3 %collective-permute-start = (f32[128,256]{1,0:T(8,128)S(1)}, f32[128,256]{1,0:T(8,128)S(1)}, u32[]{:S(2)}, u32[]{:S(2)}) collective-permute-start(f32[128,256]{1,0:T(8,128)S(1)} %get-tuple-element.25), channel_id=1, source_target_pairs={{32,64},{96,128},{160,192},{224,256},{288,320},{352,384},{416,448}... | collective-permute-start | bytes 393224 | tf_op jit(solution)/shard_map/ppermute | solution.py:303
  41.6 4.4 %collective-permute-start.1 = (f32[128,256]{1,0:T(8,128)S(1)}, f32[128,256]{1,0:T(8,128)S(1)}, u32[]{:S(2)}, u32[]{:S(2)}) collective-permute-start(f32[128,256]{1,0:T(8,128)S(1)} %get-tuple-element.26), channel_id=1, source_target_pairs={{0,32},{64,96},{128,160},{192,224},{256,288},{320,352},{384,416},{... | collective-permute-start | bytes 393224 | tf_op jit(solution)/shard_map/ppermute | solution.py:303
  70.6 10.7 %collective-permute-start.2 = (f32[128,256]{1,0:T(8,128)S(1)}, f32[128,256]{1,0:T(8,128)S(1)}, u32[]{:S(2)}, u32[]{:S(2)}) collective-permute-start(f32[128,256]{1,0:T(8,128)S(1)} %get-tuple-element.30.y_ref), channel_id=1, source_target_pairs={{64,128},{192,256},{320,384},{448,480},{416,352},{288,224},{160,96... | collective-permute-start | bytes 393224 | tf_op jit(solution)/shard_map/ppermute | solution.py:303
  73.3 10.9 %collective-permute-start.3 = (f32[128,256]{1,0:T(8,128)S(1)}, f32[128,256]{1,0:T(8,128)S(1)}, u32[]{:S(2)}, u32[]{:S(2)}) collective-permute-start(f32[128,256]{1,0:T(8,128)S(1)} %get-tuple-element.31.x_ref), channel_id=1, source_target_pairs={{0,64},{128,192},{256,320},{384,448},{480,416},{352,288},{224,160}... | collective-permute-start | bytes 393224 | tf_op jit(solution)/shard_map/ppermute | solution.py:303

commit v3 on v2

--- a/solution.py
+++ b/solution.py
@@ -289,14 +289,17 @@
     )(*inputs)
 
 
-def from_all(x, axes):
+def from_all(x, axes, first=0):
     count = lax.axis_size(axes)
     copies = jnp.broadcast_to(x[None], (count, *x.shape))
-    return lax.all_to_all(copies, axes, 0, 0, tiled=True)
+    order = [(first + i) % count for i in range(count)]
+    groups = [order] if first else None
+    return lax.all_to_all(copies, axes, 0, 0, tiled=True, axis_index_groups=groups)
 
 
 def row_parts(x):
-    return from_all(ordered_sum(from_all(x, ("half", "near"))), "far")
+    near = ordered_sum(from_all(x, ("half", "near")))
+    return from_all(near, "far", lax.axis_size("far") // 2)
 
 
 def exchange(x, edges):

time: 114 us -> 107 us (0.939)
  the two profiles are of different devices: /device:TPU:16 before, /device:TPU:24 now
where the time goes in v3:
time: 107 us
  blocking collectives  58.5 us (55%)
  starting transfers between devices  32.4 us (30%)
  waiting for transfers between devices  9.79 us (9%)
  Pallas kernels  4.46 us (4%)
  local copies, waits for them, and re-layouts  1.64 us (2%)
    all_to_all x5, blocking collectives, from_all(): lax.all_to_all(copies, axes, 0, 0, tiled=True, axis_index_groups=groups)  58.5 us
    all_to_all x1, starting transfers between devices, from_all(): lax.all_to_all(copies, axes, 0, 0, tiled=True, axis_index_groups=groups)  17.5 us
    ppermute x4, starting transfers between devices, exchange(): return lax.ppermute(x, 'pair', edges + [(j, i) for i, j in edges])  15 us
    ppermute x4, waiting for transfers between devices, exchange(): return lax.ppermute(x, 'pair', edges + [(j, i) for i, j in edges])  5.89 us
    pallas_call x6, Pallas kernels, call(): pl.pallas_call(kernel, in_specs=[pl.BlockSpec(memory_space=pltpu.SMEM)] *...  4.46 us
    all_to_all x1, waiting for transfers between devices, from_all(): lax.all_to_all(copies, axes, 0, 0, tiled=True, axis_index_groups=groups)  3.9 us
  transfers between devices with their start and end apart: 5, of which 4 were waited for; matrix products, arithmetic and copies ran while one was open for 0% of the time, Pallas kernels for 0%

profile of v3, /device:TPU:24, one launch (start us, length us, event | category | flops | bytes accessed | tf_op | source)
XLA Modules:
  0.0 107.0 jit_solution(16716098924948062353)
XLA Ops:
  0.0 0.0 copy-start
  0.0 0.9 copy-done
  1.0 1.1 %shard_map.17 = (f32[128,256]{1,0:T(8,128)S(1)}, f32[128,256]{1,0:T(8,128)S(1)}, f32[24,128]{1,0:T(8,128)S(1)}) custom-call(f32[128,512]{1,0:T(8,128)S(1)} %copy-done), custom_call_target="tpu_custom_call" | custom-call | tf_op jit(solution)/shard_map/pallas_call | solution.py:283
  2.1 8.7 %all_to_all.30 = f32[4,24,128]{2,1,0:T(8,128)S(1)} all-to-all(f32[4,24,128]{2,1,0:T(8,128)S(1)} %broadcast_in_dim.18), channel_id=1, replica_groups=mesh['pair'=16,'half'=2,'far'=8,'near'=2] {'half','near'}, dimensions={0} | all-to-all | bytes 98304 | tf_op jit(solution)/shard_map/all_to_all | solution.py:297
  10.8 0.7 broadcast_in_dim.20
  11.5 17.5 %all-to-all-start.1 = ((f32[8,24,128]{2,1,0:T(8,128)}), f32[8,24,128]{2,1,0:T(8,128)S(1)}, u32[]{:S(2)}, u32[]{:S(2)}) async-start(f32[8,24,128]{2,1,0:T(8,128)} %broadcast_in_dim.20), calls=%async_computation.1 | async-start | bytes 196608 | tf_op jit(solution)/shard_map/all_to_all | solution.py:297
  29.0 3.9 %all-to-all-done.1.parts_ref = f32[8,24,128]{2,1,0:T(8,128)S(1)} async-done(((f32[8,24,128]{2,1,0:T(8,128)}), f32[8,24,128]{2,1,0:T(8,128)S(1)}, u32[]{:S(2)}, u32[]{:S(2)}) %all-to-all-start.1) | async-done | bytes 98336 | tf_op jit(solution)/shard_map/all_to_all | solution.py:297
  32.9 0.5 shard_map.18
  33.3 1.9 %collective-permute-start = (f32[128,256]{1,0:T(8,128)S(1)}, f32[128,256]{1,0:T(8,128)S(1)}, u32[]{:S(2)}, u32[]{:S(2)}) collective-permute-start(f32[128,256]{1,0:T(8,128)S(1)} %get-tuple-element.25), channel_id=1, source_target_pairs={{32,64},{96,128},{160,192},{224,256},{288,320},{352,384},{416,448}... | collective-permute-start | bytes 393224 | tf_op jit(solution)/shard_map/ppermute | solution.py:306
  35.3 4.4 %collective-permute-start.1 = (f32[128,256]{1,0:T(8,128)S(1)}, f32[128,256]{1,0:T(8,128)S(1)}, u32[]{:S(2)}, u32[]{:S(2)}) collective-permute-start(f32[128,256]{1,0:T(8,128)S(1)} %get-tuple-element.26), channel_id=1, source_target_pairs={{0,32},{64,96},{128,160},{192,224},{256,288},{320,352},{384,416},{... | collective-permute-start | bytes 393224 | tf_op jit(solution)/shard_map/ppermute | solution.py:306
  39.7 0.0 collective-permute-done.odd_ref
  39.7 1.0 collective-permute-done.1.even_ref
  40.6 0.2 shard_map.19
  40.9 7.2 %all_to_all.31 = f32[4,24,128]{2,1,0:T(8,128)S(1)} all-to-all(f32[4,24,128]{2,1,0:T(8,128)S(1)} %broadcast_in_dim.21), channel_id=1, replica_groups=mesh['pair'=16,'half'=2,'far'=8,'near'=2] {'half','near'}, dimensions={0} | all-to-all | bytes 98304 | tf_op jit(solution)/shard_map/all_to_all | solution.py:297
  48.1 16.5 %all_to_all.32.parts_ref = f32[8,24,128]{2,1,0:T(8,128)S(1)} all-to-all(f32[8,24,128]{2,1,0:T(8,128)S(1)} %broadcast_in_dim.23), channel_id=1, replica_groups={{8,10,12,14,0,2,4,6},{9,11,13,15,1,3,5,7},{24,26,28,30,16,18,20,22},{25..., dimensions={0} | all-to-all | bytes 196608 | tf_op jit(solution)/shard_map/all_to_all | solution.py:297
  64.6 0.5 shard_map.20
  65.1 6.7 %collective-permute-start.2 = (f32[128,256]{1,0:T(8,128)S(1)}, f32[128,256]{1,0:T(8,128)S(1)}, u32[]{:S(2)}, u32[]{:S(2)}) collective-permute-start(f32[128,256]{1,0:T(8,128)S(1)} %get-tuple-element.30.y_ref), channel_id=1, source_target_pairs={{64,128},{192,256},{320,384},{448,480},{416,352},{288,224},{160,96... | collective-permute-start | bytes 393224 | tf_op jit(solution)/shard_map/ppermute | solution.py:306
  71.8 1.9 %collective-permute-start.3 = (f32[128,256]{1,0:T(8,128)S(1)}, f32[128,256]{1,0:T(8,128)S(1)}, u32[]{:S(2)}, u32[]{:S(2)}) collective-permute-start(f32[128,256]{1,0:T(8,128)S(1)} %get-tuple-element.31.x_ref), channel_id=1, source_target_pairs={{0,64},{128,192},{256,320},{384,448},{480,416},{352,288},{224,160}... | collective-permute-start | bytes 393224 | tf_op jit(solution)/shard_map/ppermute | solution.py:306
  73.7 1.8 %collective-permute-done.2.y_in_ref = f32[128,256]{1,0:T(8,128)S(1)} collective-permute-done((f32[128,256]{1,0:T(8,128)S(1)}, f32[128,256]{1,0:T(8,128)S(1)}, u32[]{:S(2)}, u32[]{:S(2)}) %collective-permute-start.2) | collective-permute-done | bytes 131104 | tf_op jit(solution)/shard_map/ppermute | solution.py:306
  75.6 3.1 %collective-permute-done.3.x_in_ref = f32[128,256]{1,0:T(8,128)S(1)} collective-permute-done((f32[128,256]{1,0:T(8,128)S(1)}, f32[128,256]{1,0:T(8,128)S(1)}, u32[]{:S(2)}, u32[]{:S(2)}) %collective-permute-start.3) | collective-permute-done | bytes 131104 | tf_op jit(solution)/shard_map/ppermute | solution.py:306
  78.7 0.4 shard_map.21
  79.1 7.3 %all_to_all.33 = f32[4,48,128]{2,1,0:T(8,128)S(1)} all-to-all(f32[4,48,128]{2,1,0:T(8,128)S(1)} %broadcast_in_dim.48), channel_id=1, replica_groups=mesh['pair'=16,'half'=2,'far'=8,'near'=2] {'half','near'}, dimensions={0} | all-to-all | bytes 196608 | tf_op jit(solution)/shard_map/all_to_all | solution.py:297
  86.4 18.8 %all_to_all.34.parts_ref = f32[8,48,128]{2,1,0:T(8,128)S(1)} all-to-all(f32[8,48,128]{2,1,0:T(8,128)S(1)} %broadcast_in_dim.50), channel_id=1, replica_groups={{8,10,12,14,0,2,4,6},{9,11,13,15,1,3,5,7},{24,26,28,30,16,18,20,22},{25..., dimensions={0} | all-to-all | bytes 393216 | tf_op jit(solution)/shard_map/all_to_all | solution.py:297
  105.2 1.7 %shard_map.22 = f32[128,512]{1,0:T(8,128)} custom-call(s32[1,1]{1,0:T(1,128)} %bitcast.place_ref, f32[128,256]{1,0:T(8,128)S(1)} %get-tuple-element.32.top_before_ref, f32[128,256]{1,0:T(8,128)S(1)} %get-tuple-element.33.bottom_before_ref, f32[128,256]{1,0:T(8,128)S(1)} %get-tuple-element.34.top_after_ref, ...), custom_call_target="tpu_custom_call" | custom-call | tf_op jit(solution)/shard_map/pallas_call | solution.py:283
  (8 shorter events, 0.1 us)
Async XLA Ops:
  0.0 0.9 copy-start
  11.5 21.4 %all-to-all-start.1 = ((f32[8,24,128]{2,1,0:T(8,128)}), f32[8,24,128]{2,1,0:T(8,128)S(1)}, u32[]{:S(2)}, u32[]{:S(2)}) async-start(f32[8,24,128]{2,1,0:T(8,128)} %broadcast_in_dim.20), calls=%async_computation.1 | async-start | bytes 196608 | tf_op jit(solution)/shard_map/all_to_all | solution.py:297
  33.3 6.3 %collective-permute-start = (f32[128,256]{1,0:T(8,128)S(1)}, f32[128,256]{1,0:T(8,128)S(1)}, u32[]{:S(2)}, u32[]{:S(2)}) collective-permute-start(f32[128,256]{1,0:T(8,128)S(1)} %get-tuple-element.25), channel_id=1, source_target_pairs={{32,64},{96,128},{160,192},{224,256},{288,320},{352,384},{416,448}... | collective-permute-start | bytes 393224 | tf_op jit(solution)/shard_map/ppermute | solution.py:306
  35.3 5.4 %collective-permute-start.1 = (f32[128,256]{1,0:T(8,128)S(1)}, f32[128,256]{1,0:T(8,128)S(1)}, u32[]{:S(2)}, u32[]{:S(2)}) collective-permute-start(f32[128,256]{1,0:T(8,128)S(1)} %get-tuple-element.26), channel_id=1, source_target_pairs={{0,32},{64,96},{128,160},{192,224},{256,288},{320,352},{384,416},{... | collective-permute-start | bytes 393224 | tf_op jit(solution)/shard_map/ppermute | solution.py:306
  65.1 10.5 %collective-permute-start.2 = (f32[128,256]{1,0:T(8,128)S(1)}, f32[128,256]{1,0:T(8,128)S(1)}, u32[]{:S(2)}, u32[]{:S(2)}) collective-permute-start(f32[128,256]{1,0:T(8,128)S(1)} %get-tuple-element.30.y_ref), channel_id=1, source_target_pairs={{64,128},{192,256},{320,384},{448,480},{416,352},{288,224},{160,96... | collective-permute-start | bytes 393224 | tf_op jit(solution)/shard_map/ppermute | solution.py:306
  71.8 6.9 %collective-permute-start.3 = (f32[128,256]{1,0:T(8,128)S(1)}, f32[128,256]{1,0:T(8,128)S(1)}, u32[]{:S(2)}, u32[]{:S(2)}) collective-permute-start(f32[128,256]{1,0:T(8,128)S(1)} %get-tuple-element.31.x_ref), channel_id=1, source_target_pairs={{0,64},{128,192},{256,320},{384,448},{480,416},{352,288},{224,160}... | collective-permute-start | bytes 393224 | tf_op jit(solution)/shard_map/ppermute | solution.py:306

commit v4 on v3

--- a/solution.py
+++ b/solution.py
@@ -184,8 +184,18 @@
     return [pl.ds(start, CHUNK) for start in range(0, ref.shape[0], CHUNK)]
 
 
-def start_kernel(work_ref, top_ref, bottom_ref, band_ref):
+def start_kernel(place_ref, work_hbm, top_ref, bottom_ref, band_ref, work_ref, sems):
+    rows = work_ref.shape[0]
+    size = rows // sems.shape[0]
+    copies = []
+    for i in range(sems.shape[0]):
+        part = pl.ds(i * size, size)
+        copies.append(pltpu.make_async_copy(work_hbm.at[part], work_ref.at[part], sems.at[i]))
+        copies[-1].start()
+
     def read(start):
+        if start % size == 0:
+            copies[start // size].wait()
         row = pl.ds(start, CHUNK)
         top = to_cycle(work_ref[row, :HALF])
         bottom = reverse(to_cycle(work_ref[row, HALF:]))
@@ -193,7 +203,7 @@
         bottom_ref[row, :] = bottom
         return top, bottom
 
-    band_ref[...] = pack(bands_of(read, work_ref.shape[0]))
+    band_ref[...] = pack(bands_of(read, rows))
 
 
 def rotate_kernel(place_ref, top_ref, bottom_ref, parts_ref, kept_ref, odd_ref, even_ref):
@@ -278,13 +288,15 @@
         out_ref[row, HALF:] = from_cycle(chosen(place == count - 1, top, reverse(bottom)))
 
 
-def call(kernel, inputs, outputs, scalars=0):
+def call(kernel, inputs, outputs, scratch=(), space=pltpu.VMEM):
     spec = pl.BlockSpec(memory_space=pltpu.VMEM)
+    places = [pl.BlockSpec(memory_space=pltpu.SMEM)]
     return pl.pallas_call(
         kernel,
-        in_specs=[pl.BlockSpec(memory_space=pltpu.SMEM)] * scalars + [spec] * (len(inputs) - scalars),
+        in_specs=places + [pl.BlockSpec(memory_space=space)] * (len(inputs) - 1),
         out_specs=[spec] * len(outputs),
         out_shape=[jax.ShapeDtypeStruct(shape, jnp.float32) for shape in outputs],
+        scratch_shapes=list(scratch),
         compiler_params=pltpu.CompilerParams(vmem_limit_bytes=8 * 1024 * 1024),
     )(*inputs)
 
@@ -300,6 +312,12 @@
 def row_parts(x):
     near = ordered_sum(from_all(x, ("half", "near")))
     return from_all(near, "far", lax.axis_size("far") // 2)
+
+
+def row_parts_of_ring(x):
+    both = x + lax.ppermute(x, "half", [(0, 1), (1, 0)])
+    ring = ("far", "near")
+    return from_all(both, ring, lax.axis_size(ring) // 2)
 
 
 def exchange(x, edges):
@@ -317,21 +335,25 @@
     x_edges = list(zip(cycle[::2], cycle[1::2]))
     y_edges = list(zip(cycle[1::2], cycle[2::2] + cycle[:1]))
 
-    top, bottom, band = call(start_kernel, [snapshots], [block, block, packed])
+    top, bottom, band = call(
+        start_kernel,
+        [place, snapshots],
+        [block, block, packed],
+        [pltpu.VMEM((rows, 2 * HALF), jnp.float32), pltpu.SemaphoreType.DMA((4,))],
+        pltpu.HBM,
+    )
     kept, odd, even = call(
-        rotate_kernel, [place, top, bottom, row_parts(band)], [block] * 3, 1
+        rotate_kernel, [place, top, bottom, row_parts_of_ring(band)], [block] * 3
     )
     top, bottom, band = call(
         functools.partial(arrive_kernel, count),
         [place, kept, exchange(odd, odd_edges), exchange(even, even_edges)],
         [block, block, packed],
-        1,
     )
     y, x = call(
         functools.partial(rotate_far_kernel, count),
-        [place, top, bottom, row_parts(band)],
+        [place, top, bottom, row_parts_of_ring(band)],
         [block] * 2,
-        1,
     )
     y_in = exchange(y, y_edges)
     x_in = exchange(x, x_edges)
@@ -339,13 +361,11 @@
         functools.partial(arrive_far_kernel, count),
         [place, y, x, y_in, x_in],
         [block] * 4 + [(2 * PACKED_ROWS, LANES)],
-        1,
     )
     (out,) = call(
         functools.partial(finish_kernel, count),
         [place, *blocks, row_parts(band)],
         [(rows, 2 * HALF)],
-        1,
     )
     return out
 

time: 107 us -> 111 us (1.037)
  the two profiles are of different devices: /device:TPU:24 before, /device:TPU:4 now
where the time goes in v4:
time: 111 us; the launch traced here: 110 us
  blocking collectives  71.7 us (65%)
  starting transfers between devices  18.5 us (17%)
  waiting for transfers between devices  14.3 us (13%)
  Pallas kernels  4.57 us (4%)
    all_to_all x4, blocking collectives, from_all(): lax.all_to_all(copies, axes, 0, 0, tiled=True, axis_index_groups=groups)  71.7 us
    ppermute x4, starting transfers between devices, exchange(): return lax.ppermute(x, 'pair', edges + [(j, i) for i, j in edges])  12.2 us
    ppermute x4, waiting for transfers between devices, exchange(): return lax.ppermute(x, 'pair', edges + [(j, i) for i, j in edges])  9.31 us
    ppermute x2, starting transfers between devices, row_parts_of_ring(): both = x + lax.ppermute(x, 'half', [(0, 1), (1, 0)])  6.21 us
    ppermute x2, waiting for transfers between devices, row_parts_of_ring(): both = x + lax.ppermute(x, 'half', [(0, 1), (1, 0)])  4.95 us
    pallas_call x6, Pallas kernels, call(): pl.pallas_call(kernel, in_specs=places + [pl.BlockSpec(memory_space=space...  4.57 us
  transfers between devices with their start and end apart: 6, of which 5 were waited for; matrix products, arithmetic and copies ran while one was open for 0% of the time, Pallas kernels for 0%

profile of v4, /device:TPU:4, one launch (start us, length us, event | category | flops | bytes accessed | tf_op | source)
XLA Modules:
  0.0 110.1 jit_solution(12577327548293153696)
XLA Ops:
  0.0 0.0 copy-start
  0.0 0.9 copy-done
  1.0 1.2 %shard_map.17 = (f32[128,256]{1,0:T(8,128)S(1)}, f32[128,256]{1,0:T(8,128)S(1)}, f32[24,128]{1,0:T(8,128)S(1)}) custom-call(s32[1,1]{1,0:T(1,128)} %bitcast.place_ref, f32[128,512]{1,0:T(8,128)S(1)} %copy-done), custom_call_target="tpu_custom_call" | custom-call | tf_op jit(solution)/shard_map/pallas_call | solution.py:294
  2.2 3.1 %collective-permute-start = (f32[24,128]{1,0:T(8,128)S(1)}, f32[24,128]{1,0:T(8,128)S(1)}, u32[]{:S(2)}, u32[]{:S(2)}) collective-permute-start(f32[24,128]{1,0:T(8,128)S(1)} %get-tuple-element.23), channel_id=1, source_target_pairs={{0,16},{16,0},{1,17},{17,1},{2,18},{18,2},{3,19},{19,3},{4,20},{20... | collective-permute-start | bytes 36872 | tf_op jit(solution)/shard_map/ppermute | solution.py:318
  5.3 2.5 %collective-permute-done = f32[24,128]{1,0:T(8,128)S(1)} collective-permute-done((f32[24,128]{1,0:T(8,128)S(1)}, f32[24,128]{1,0:T(8,128)S(1)}, u32[]{:S(2)}, u32[]{:S(2)}) %collective-permute-start) | collective-permute-done | bytes 12320 | tf_op jit(solution)/shard_map/ppermute | solution.py:318
  7.8 26.8 %all_to_all.20.parts_ref = f32[16,24,128]{2,1,0:T(8,128)S(1)} all-to-all(f32[16,24,128]{2,1,0:T(8,128)S(1)} %broadcast_in_dim.10), channel_id=1, replica_groups={{8,9,10,11,12,13,14,15,0,1,2,3,4,5,6,7},{24,25,26,27,28,29,30,31,16,17,..., dimensions={0} | all-to-all | bytes 393216 | tf_op jit(solution)/shard_map/all_to_all | solution.py:309
  34.6 0.5 shard_map.18
  35.1 2.3 %collective-permute-start.1 = (f32[128,256]{1,0:T(8,128)S(1)}, f32[128,256]{1,0:T(8,128)S(1)}, u32[]{:S(2)}, u32[]{:S(2)}) collective-permute-start(f32[128,256]{1,0:T(8,128)S(1)} %get-tuple-element.25), channel_id=1, source_target_pairs={{32,64},{96,128},{160,192},{224,256},{288,320},{352,384},{416,448}... | collective-permute-start | bytes 393224 | tf_op jit(solution)/shard_map/ppermute | solution.py:324
  37.4 3.2 %collective-permute-start.2 = (f32[128,256]{1,0:T(8,128)S(1)}, f32[128,256]{1,0:T(8,128)S(1)}, u32[]{:S(2)}, u32[]{:S(2)}) collective-permute-start(f32[128,256]{1,0:T(8,128)S(1)} %get-tuple-element.26), channel_id=1, source_target_pairs={{0,32},{64,96},{128,160},{192,224},{256,288},{320,352},{384,416},{... | collective-permute-start | bytes 393224 | tf_op jit(solution)/shard_map/ppermute | solution.py:324
  40.6 4.4 %collective-permute-done.1.odd_ref = f32[128,256]{1,0:T(8,128)S(1)} collective-permute-done((f32[128,256]{1,0:T(8,128)S(1)}, f32[128,256]{1,0:T(8,128)S(1)}, u32[]{:S(2)}, u32[]{:S(2)}) %collective-permute-start.1) | collective-permute-done | bytes 131104 | tf_op jit(solution)/shard_map/ppermute | solution.py:324
  45.0 0.0 collective-permute-done.2.even_ref
  45.0 0.2 shard_map.19
  45.2 3.1 %collective-permute-start.3 = (f32[24,128]{1,0:T(8,128)S(1)}, f32[24,128]{1,0:T(8,128)S(1)}, u32[]{:S(2)}, u32[]{:S(2)}) collective-permute-start(f32[24,128]{1,0:T(8,128)S(1)} %get-tuple-element.29), channel_id=1, source_target_pairs={{0,16},{16,0},{1,17},{17,1},{2,18},{18,2},{3,19},{19,3},{4,20},{20... | collective-permute-start | bytes 36872 | tf_op jit(solution)/shard_map/ppermute | solution.py:318
  48.4 2.5 %collective-permute-done.3 = f32[24,128]{1,0:T(8,128)S(1)} collective-permute-done((f32[24,128]{1,0:T(8,128)S(1)}, f32[24,128]{1,0:T(8,128)S(1)}, u32[]{:S(2)}, u32[]{:S(2)}) %collective-permute-start.3) | collective-permute-done | bytes 12320 | tf_op jit(solution)/shard_map/ppermute | solution.py:318
  50.9 18.3 %all_to_all.21.parts_ref = f32[16,24,128]{2,1,0:T(8,128)S(1)} all-to-all(f32[16,24,128]{2,1,0:T(8,128)S(1)} %broadcast_in_dim.11), channel_id=1, replica_groups={{8,9,10,11,12,13,14,15,0,1,2,3,4,5,6,7},{24,25,26,27,28,29,30,31,16,17,..., dimensions={0} | all-to-all | bytes 393216 | tf_op jit(solution)/shard_map/all_to_all | solution.py:309
  69.2 0.5 shard_map.20
  69.7 4.8 %collective-permute-start.4 = (f32[128,256]{1,0:T(8,128)S(1)}, f32[128,256]{1,0:T(8,128)S(1)}, u32[]{:S(2)}, u32[]{:S(2)}) collective-permute-start(f32[128,256]{1,0:T(8,128)S(1)} %get-tuple-element.30.y_ref), channel_id=1, source_target_pairs={{64,128},{192,256},{320,384},{448,480},{416,352},{288,224},{160,96... | collective-permute-start | bytes 393224 | tf_op jit(solution)/shard_map/ppermute | solution.py:324
  74.5 1.9 %collective-permute-start.5 = (f32[128,256]{1,0:T(8,128)S(1)}, f32[128,256]{1,0:T(8,128)S(1)}, u32[]{:S(2)}, u32[]{:S(2)}) collective-permute-start(f32[128,256]{1,0:T(8,128)S(1)} %get-tuple-element.31.x_ref), channel_id=1, source_target_pairs={{0,64},{128,192},{256,320},{384,448},{480,416},{352,288},{224,160}... | collective-permute-start | bytes 393224 | tf_op jit(solution)/shard_map/ppermute | solution.py:324
  76.5 3.7 %collective-permute-done.4.y_in_ref = f32[128,256]{1,0:T(8,128)S(1)} collective-permute-done((f32[128,256]{1,0:T(8,128)S(1)}, f32[128,256]{1,0:T(8,128)S(1)}, u32[]{:S(2)}, u32[]{:S(2)}) %collective-permute-start.4) | collective-permute-done | bytes 131104 | tf_op jit(solution)/shard_map/ppermute | solution.py:324
  80.2 1.2 %collective-permute-done.5.x_in_ref = f32[128,256]{1,0:T(8,128)S(1)} collective-permute-done((f32[128,256]{1,0:T(8,128)S(1)}, f32[128,256]{1,0:T(8,128)S(1)}, u32[]{:S(2)}, u32[]{:S(2)}) %collective-permute-start.5) | collective-permute-done | bytes 131104 | tf_op jit(solution)/shard_map/ppermute | solution.py:324
  81.4 0.4 shard_map.21
  81.8 8.8 %all_to_all.22 = f32[4,48,128]{2,1,0:T(8,128)S(1)} all-to-all(f32[4,48,128]{2,1,0:T(8,128)S(1)} %broadcast_in_dim.12), channel_id=1, replica_groups=mesh['pair'=16,'half'=2,'far'=8,'near'=2] {'half','near'}, dimensions={0} | all-to-all | bytes 196608 | tf_op jit(solution)/shard_map/all_to_all | solution.py:309
  90.7 17.7 %all_to_all.23.parts_ref = f32[8,48,128]{2,1,0:T(8,128)S(1)} all-to-all(f32[8,48,128]{2,1,0:T(8,128)S(1)} %broadcast_in_dim.14), channel_id=1, replica_groups={{8,10,12,14,0,2,4,6},{9,11,13,15,1,3,5,7},{24,26,28,30,16,18,20,22},{25..., dimensions={0} | all-to-all | bytes 393216 | tf_op jit(solution)/shard_map/all_to_all | solution.py:309
  108.4 1.7 %shard_map.22 = f32[128,512]{1,0:T(8,128)} custom-call(s32[1,1]{1,0:T(1,128)} %bitcast.place_ref, f32[128,256]{1,0:T(8,128)S(1)} %get-tuple-element.32.top_before_ref, f32[128,256]{1,0:T(8,128)S(1)} %get-tuple-element.33.bottom_before_ref, f32[128,256]{1,0:T(8,128)S(1)} %get-tuple-element.34.top_after_ref, ...), custom_call_target="tpu_custom_call" | custom-call | tf_op jit(solution)/shard_map/pallas_call | solution.py:294
  (7 shorter events, 0.1 us)
Async XLA Ops:
  0.0 0.9 copy-start
  2.2 5.6 %collective-permute-start = (f32[24,128]{1,0:T(8,128)S(1)}, f32[24,128]{1,0:T(8,128)S(1)}, u32[]{:S(2)}, u32[]{:S(2)}) collective-permute-start(f32[24,128]{1,0:T(8,128)S(1)} %get-tuple-element.23), channel_id=1, source_target_pairs={{0,16},{16,0},{1,17},{17,1},{2,18},{18,2},{3,19},{19,3},{4,20},{20... | collective-permute-start | bytes 36872 | tf_op jit(solution)/shard_map/ppermute | solution.py:318
  35.1 9.9 %collective-permute-start.1 = (f32[128,256]{1,0:T(8,128)S(1)}, f32[128,256]{1,0:T(8,128)S(1)}, u32[]{:S(2)}, u32[]{:S(2)}) collective-permute-start(f32[128,256]{1,0:T(8,128)S(1)} %get-tuple-element.25), channel_id=1, source_target_pairs={{32,64},{96,128},{160,192},{224,256},{288,320},{352,384},{416,448}... | collective-permute-start | bytes 393224 | tf_op jit(solution)/shard_map/ppermute | solution.py:324
  37.4 7.6 %collective-permute-start.2 = (f32[128,256]{1,0:T(8,128)S(1)}, f32[128,256]{1,0:T(8,128)S(1)}, u32[]{:S(2)}, u32[]{:S(2)}) collective-permute-start(f32[128,256]{1,0:T(8,128)S(1)} %get-tuple-element.26), channel_id=1, source_target_pairs={{0,32},{64,96},{128,160},{192,224},{256,288},{320,352},{384,416},{... | collective-permute-start | bytes 393224 | tf_op jit(solution)/shard_map/ppermute | solution.py:324
  45.2 5.6 %collective-permute-start.3 = (f32[24,128]{1,0:T(8,128)S(1)}, f32[24,128]{1,0:T(8,128)S(1)}, u32[]{:S(2)}, u32[]{:S(2)}) collective-permute-start(f32[24,128]{1,0:T(8,128)S(1)} %get-tuple-element.29), channel_id=1, source_target_pairs={{0,16},{16,0},{1,17},{17,1},{2,18},{18,2},{3,19},{19,3},{4,20},{20... | collective-permute-start | bytes 36872 | tf_op jit(solution)/shard_map/ppermute | solution.py:318
  69.7 10.5 %collective-permute-start.4 = (f32[128,256]{1,0:T(8,128)S(1)}, f32[128,256]{1,0:T(8,128)S(1)}, u32[]{:S(2)}, u32[]{:S(2)}) collective-permute-start(f32[128,256]{1,0:T(8,128)S(1)} %get-tuple-element.30.y_ref), channel_id=1, source_target_pairs={{64,128},{192,256},{320,384},{448,480},{416,352},{288,224},{160,96... | collective-permute-start | bytes 393224 | tf_op jit(solution)/shard_map/ppermute | solution.py:324
  74.5 6.9 %collective-permute-start.5 = (f32[128,256]{1,0:T(8,128)S(1)}, f32[128,256]{1,0:T(8,128)S(1)}, u32[]{:S(2)}, u32[]{:S(2)}) collective-permute-start(f32[128,256]{1,0:T(8,128)S(1)} %get-tuple-element.31.x_ref), channel_id=1, source_target_pairs={{0,64},{128,192},{256,320},{384,448},{480,416},{352,288},{224,160}... | collective-permute-start | bytes 393224 | tf_op jit(solution)/shard_map/ppermute | solution.py:324

commit v5 on v3

--- a/solution.py
+++ b/solution.py
@@ -184,7 +184,7 @@
     return [pl.ds(start, CHUNK) for start in range(0, ref.shape[0], CHUNK)]
 
 
-def start_kernel(work_ref, top_ref, bottom_ref, band_ref):
+def start_kernel(place_ref, work_ref, top_ref, bottom_ref, band_ref):
     def read(start):
         row = pl.ds(start, CHUNK)
         top = to_cycle(work_ref[row, :HALF])
@@ -224,7 +224,7 @@
     band_ref[...] = pack(bands_of(read, kept_ref.shape[0]))
 
 
-def rotate_far_kernel(count, place_ref, top_ref, bottom_ref, parts_ref, y_ref, x_ref):
+def rotate_far_kernel(count, place_ref, top_ref, bottom_ref, parts_ref, x_ref, y_ref, late_ref):
     place = place_ref[0, 0]
     low = place % 4 < 2
     matrices = wide(three_matrices(ordered_sum(parts_ref)))
@@ -233,19 +233,28 @@
         flip = reverse(chosen(place == 0, bottom, top))
         upper = chosen((place == 0) | (place == count - 1), flip, top)
         lower = chosen(place == 0, top, bottom)
-        x_ref[row, :] = chosen(low, upper, lower)
+        x = chosen(low, upper, lower)
+        x_ref[row, :] = x
         y_ref[row, :] = chosen(low, lower, upper)
-
-
-def arrive_far_kernel(count, place_ref, y_ref, x_ref, y_in_ref, x_in_ref, *refs):
+        late_ref[row, :] = x
+
+
+def late_edges(count):
+    middle = count // 2
+    return [(middle, middle + 2), (middle - 1, middle - 3)]
+
+
+def arrive_far_kernel(count, place_ref, x_ref, y_ref, late_ref, x_in_ref, y_in_ref, late_in_ref, *refs):
     before_refs, after_refs, band_ref = refs[:2], refs[2:4], refs[4]
     place = place_ref[0, 0]
     low = place % 4 < 2
     start_end, last_end = place == 0, place == count - 1
+    late = functools.reduce(jnp.logical_or, [place == i for i in sum(late_edges(count), ())])
 
     def read_before(start):
         row = pl.ds(start, CHUNK)
-        x, y, x_in, y_in = x_ref[row, :], y_ref[row, :], x_in_ref[row, :], y_in_ref[row, :]
+        x, y, y_in = x_ref[row, :], y_ref[row, :], y_in_ref[row, :]
+        x_in = chosen(late, late_in_ref[row, :], x_in_ref[row, :])
         top = chosen(start_end, y, chosen(low, y_in, x_in))
         bottom = chosen(start_end, y_in, chosen(low, y, x))
         before_refs[0][row, :] = top
@@ -254,7 +263,8 @@
 
     def read_after(start):
         row = pl.ds(start, CHUNK)
-        x, y, x_in, y_in = x_ref[row, :], y_ref[row, :], x_in_ref[row, :], y_in_ref[row, :]
+        x, y, y_in = x_ref[row, :], y_ref[row, :], y_in_ref[row, :]
+        x_in = chosen(late, late_in_ref[row, :], x_in_ref[row, :])
         top = chosen(low, x, chosen(last_end, y_in, y))
         bottom = chosen(low, x_in, chosen(last_end, y, y_in))
         after_refs[0][row, :] = top
@@ -278,11 +288,11 @@
         out_ref[row, HALF:] = from_cycle(chosen(place == count - 1, top, reverse(bottom)))
 
 
-def call(kernel, inputs, outputs, scalars=0):
+def call(kernel, inputs, outputs):
     spec = pl.BlockSpec(memory_space=pltpu.VMEM)
     return pl.pallas_call(
         kernel,
-        in_specs=[pl.BlockSpec(memory_space=pltpu.SMEM)] * scalars + [spec] * (len(inputs) - scalars),
+        in_specs=[pl.BlockSpec(memory_space=pltpu.SMEM)] + [spec] * (len(inputs) - 1),
         out_specs=[spec] * len(outputs),
         out_shape=[jax.ShapeDtypeStruct(shape, jnp.float32) for shape in outputs],
         compiler_params=pltpu.CompilerParams(vmem_limit_bytes=8 * 1024 * 1024),
@@ -317,35 +327,32 @@
     x_edges = list(zip(cycle[::2], cycle[1::2]))
     y_edges = list(zip(cycle[1::2], cycle[2::2] + cycle[:1]))
 
-    top, bottom, band = call(start_kernel, [snapshots], [block, block, packed])
+    top, bottom, band = call(start_kernel, [place, snapshots], [block, block, packed])
     kept, odd, even = call(
-        rotate_kernel, [place, top, bottom, row_parts(band)], [block] * 3, 1
+        rotate_kernel, [place, top, bottom, row_parts(band)], [block] * 3
     )
     top, bottom, band = call(
         functools.partial(arrive_kernel, count),
         [place, kept, exchange(odd, odd_edges), exchange(even, even_edges)],
         [block, block, packed],
-        1,
-    )
-    y, x = call(
+    )
+    x, y, late = call(
         functools.partial(rotate_far_kernel, count),
         [place, top, bottom, row_parts(band)],
-        [block] * 2,
-        1,
-    )
+        [block] * 3,
+    )
+    x_in = exchange(x, [edge for edge in x_edges if edge not in late_edges(count)])
     y_in = exchange(y, y_edges)
-    x_in = exchange(x, x_edges)
+    late_in = exchange(late, late_edges(count))
     *blocks, band = call(
         functools.partial(arrive_far_kernel, count),
-        [place, y, x, y_in, x_in],
+        [place, x, y, late, x_in, y_in, late_in],
         [block] * 4 + [(2 * PACKED_ROWS, LANES)],
-        1,
     )
     (out,) = call(
         functools.partial(finish_kernel, count),
         [place, *blocks, row_parts(band)],
         [(rows, 2 * HALF)],
-        1,
     )
     return out
 

time: 107 us -> 107 us (level)
  the two profiles are of different devices: /device:TPU:24 before, /device:TPU:4 now
where the time goes in v5:
time: 107 us
  blocking collectives  79.5 us (74%)
  starting transfers between devices  12.1 us (11%)
  waiting for transfers between devices  9.3 us (9%)
  Pallas kernels  4.46 us (4%)
    all_to_all x6, blocking collectives, from_all(): lax.all_to_all(copies, axes, 0, 0, tiled=True, axis_index_groups=groups)  79.5 us
    ppermute x5, starting transfers between devices, exchange(): return lax.ppermute(x, 'pair', edges + [(j, i) for i, j in edges])  12.1 us
    ppermute x5, waiting for transfers between devices, exchange(): return lax.ppermute(x, 'pair', edges + [(j, i) for i, j in edges])  9.3 us
    pallas_call x6, Pallas kernels, call(): pl.pallas_call(kernel, in_specs=[pl.BlockSpec(memory_space=pltpu.SMEM)] +...  4.46 us
  transfers between devices with their start and end apart: 5, of which 3 were waited for; matrix products, arithmetic and copies ran while one was open for 0% of the time, Pallas kernels for 0%

profile of v5, /device:TPU:4, one launch (start us, length us, event | category | flops | bytes accessed | tf_op | source)
XLA Modules:
  0.0 106.6 jit_solution(6199972054208877419)
XLA Ops:
  0.0 0.0 copy-start
  0.0 0.9 copy-done
  1.0 1.1 %shard_map.17 = (f32[128,256]{1,0:T(8,128)S(1)}, f32[128,256]{1,0:T(8,128)S(1)}, f32[24,128]{1,0:T(8,128)S(1)}) custom-call(s32[1,1]{1,0:T(1,128)} %bitcast.place_ref, f32[128,512]{1,0:T(8,128)S(1)} %copy-done), custom_call_target="tpu_custom_call" | custom-call | tf_op jit(solution)/shard_map/pallas_call | solution.py:293
  2.1 8.4 %all_to_all.30 = f32[4,24,128]{2,1,0:T(8,128)S(1)} all-to-all(f32[4,24,128]{2,1,0:T(8,128)S(1)} %broadcast_in_dim.18), channel_id=1, replica_groups=mesh['pair'=16,'half'=2,'far'=8,'near'=2] {'half','near'}, dimensions={0} | all-to-all | bytes 98304 | tf_op jit(solution)/shard_map/all_to_all | solution.py:307
  10.5 21.2 %all_to_all.31.parts_ref = f32[8,24,128]{2,1,0:T(8,128)S(1)} all-to-all(f32[8,24,128]{2,1,0:T(8,128)S(1)} %broadcast_in_dim.20), channel_id=1, replica_groups={{8,10,12,14,0,2,4,6},{9,11,13,15,1,3,5,7},{24,26,28,30,16,18,20,22},{25..., dimensions={0} | all-to-all | bytes 196608 | tf_op jit(solution)/shard_map/all_to_all | solution.py:307
  31.7 0.5 shard_map.18
  32.2 2.3 %collective-permute-start = (f32[128,256]{1,0:T(8,128)S(1)}, f32[128,256]{1,0:T(8,128)S(1)}, u32[]{:S(2)}, u32[]{:S(2)}) collective-permute-start(f32[128,256]{1,0:T(8,128)S(1)} %get-tuple-element.26), channel_id=1, source_target_pairs={{32,64},{96,128},{160,192},{224,256},{288,320},{352,384},{416,448}... | collective-permute-start | bytes 393224 | tf_op jit(solution)/shard_map/ppermute | solution.py:316
  34.5 3.2 %collective-permute-start.1 = (f32[128,256]{1,0:T(8,128)S(1)}, f32[128,256]{1,0:T(8,128)S(1)}, u32[]{:S(2)}, u32[]{:S(2)}) collective-permute-start(f32[128,256]{1,0:T(8,128)S(1)} %get-tuple-element.27), channel_id=1, source_target_pairs={{0,32},{64,96},{128,160},{192,224},{256,288},{320,352},{384,416},{... | collective-permute-start | bytes 393224 | tf_op jit(solution)/shard_map/ppermute | solution.py:316
  37.7 4.4 %collective-permute-done.odd_ref = f32[128,256]{1,0:T(8,128)S(1)} collective-permute-done((f32[128,256]{1,0:T(8,128)S(1)}, f32[128,256]{1,0:T(8,128)S(1)}, u32[]{:S(2)}, u32[]{:S(2)}) %collective-permute-start) | collective-permute-done | bytes 131104 | tf_op jit(solution)/shard_map/ppermute | solution.py:316
  42.1 0.0 collective-permute-done.1.even_ref
  42.1 0.2 shard_map.19
  42.4 7.2 %all_to_all.32 = f32[4,24,128]{2,1,0:T(8,128)S(1)} all-to-all(f32[4,24,128]{2,1,0:T(8,128)S(1)} %broadcast_in_dim.21), channel_id=1, replica_groups=mesh['pair'=16,'half'=2,'far'=8,'near'=2] {'half','near'}, dimensions={0} | all-to-all | bytes 98304 | tf_op jit(solution)/shard_map/all_to_all | solution.py:307
  49.5 16.3 %all_to_all.33.parts_ref = f32[8,24,128]{2,1,0:T(8,128)S(1)} all-to-all(f32[8,24,128]{2,1,0:T(8,128)S(1)} %broadcast_in_dim.23), channel_id=1, replica_groups={{8,10,12,14,0,2,4,6},{9,11,13,15,1,3,5,7},{24,26,28,30,16,18,20,22},{25..., dimensions={0} | all-to-all | bytes 196608 | tf_op jit(solution)/shard_map/all_to_all | solution.py:307
  65.9 0.5 shard_map.20
  66.4 0.7 collective-permute-start.2
  67.1 4.0 %collective-permute-start.3 = (f32[128,256]{1,0:T(8,128)S(1)}, f32[128,256]{1,0:T(8,128)S(1)}, u32[]{:S(2)}, u32[]{:S(2)}) collective-permute-start(f32[128,256]{1,0:T(8,128)S(1)} %get-tuple-element.32.y_ref), channel_id=1, source_target_pairs={{64,128},{192,256},{320,384},{448,480},{416,352},{288,224},{160,96... | collective-permute-start | bytes 393224 | tf_op jit(solution)/shard_map/ppermute | solution.py:316
  71.1 1.9 %collective-permute-start.4 = (f32[128,256]{1,0:T(8,128)S(1)}, f32[128,256]{1,0:T(8,128)S(1)}, u32[]{:S(2)}, u32[]{:S(2)}) collective-permute-start(f32[128,256]{1,0:T(8,128)S(1)} %get-tuple-element.33.late_ref), channel_id=1, source_target_pairs={{256,320},{224,160},{320,256},{160,224},{257,321},{225,161},{321,2... | collective-permute-start | bytes 393224 | tf_op jit(solution)/shard_map/ppermute | solution.py:316
  73.0 0.0 collective-permute-done.2.x_in_ref
  73.0 4.5 %collective-permute-done.3.y_in_ref = f32[128,256]{1,0:T(8,128)S(1)} collective-permute-done((f32[128,256]{1,0:T(8,128)S(1)}, f32[128,256]{1,0:T(8,128)S(1)}, u32[]{:S(2)}, u32[]{:S(2)}) %collective-permute-start.3) | collective-permute-done | bytes 131104 | tf_op jit(solution)/shard_map/ppermute | solution.py:316
  77.5 0.4 collective-permute-done.4.late_in_ref
  77.9 0.4 shard_map.21
  78.3 7.8 %all_to_all.34 = f32[4,48,128]{2,1,0:T(8,128)S(1)} all-to-all(f32[4,48,128]{2,1,0:T(8,128)S(1)} %broadcast_in_dim.48), channel_id=1, replica_groups=mesh['pair'=16,'half'=2,'far'=8,'near'=2] {'half','near'}, dimensions={0} | all-to-all | bytes 196608 | tf_op jit(solution)/shard_map/all_to_all | solution.py:307
  86.2 18.6 %all_to_all.35.parts_ref = f32[8,48,128]{2,1,0:T(8,128)S(1)} all-to-all(f32[8,48,128]{2,1,0:T(8,128)S(1)} %broadcast_in_dim.50), channel_id=1, replica_groups={{8,10,12,14,0,2,4,6},{9,11,13,15,1,3,5,7},{24,26,28,30,16,18,20,22},{25..., dimensions={0} | all-to-all | bytes 393216 | tf_op jit(solution)/shard_map/all_to_all | solution.py:307
  104.8 1.7 %shard_map.22 = f32[128,512]{1,0:T(8,128)} custom-call(s32[1,1]{1,0:T(1,128)} %bitcast.place_ref, f32[128,256]{1,0:T(8,128)S(1)} %get-tuple-element.34.top_before_ref, f32[128,256]{1,0:T(8,128)S(1)} %get-tuple-element.35.bottom_before_ref, f32[128,256]{1,0:T(8,128)S(1)} %get-tuple-element.36.top_after_ref, ...), custom_call_target="tpu_custom_call" | custom-call | tf_op jit(solution)/shard_map/pallas_call | solution.py:293
  (9 shorter events, 0.1 us)
Async XLA Ops:
  0.0 0.9 copy-start
  32.2 9.9 %collective-permute-start = (f32[128,256]{1,0:T(8,128)S(1)}, f32[128,256]{1,0:T(8,128)S(1)}, u32[]{:S(2)}, u32[]{:S(2)}) collective-permute-start(f32[128,256]{1,0:T(8,128)S(1)} %get-tuple-element.26), channel_id=1, source_target_pairs={{32,64},{96,128},{160,192},{224,256},{288,320},{352,384},{416,448}... | collective-permute-start | bytes 393224 | tf_op jit(solution)/shard_map/ppermute | solution.py:316
  34.5 7.6 %collective-permute-start.1 = (f32[128,256]{1,0:T(8,128)S(1)}, f32[128,256]{1,0:T(8,128)S(1)}, u32[]{:S(2)}, u32[]{:S(2)}) collective-permute-start(f32[128,256]{1,0:T(8,128)S(1)} %get-tuple-element.27), channel_id=1, source_target_pairs={{0,32},{64,96},{128,160},{192,224},{256,288},{320,352},{384,416},{... | collective-permute-start | bytes 393224 | tf_op jit(solution)/shard_map/ppermute | solution.py:316
  66.4 6.6 %collective-permute-start.2 = (f32[128,256]{1,0:T(8,128)S(1)}, f32[128,256]{1,0:T(8,128)S(1)}, u32[]{:S(2)}, u32[]{:S(2)}) collective-permute-start(f32[128,256]{1,0:T(8,128)S(1)} %get-tuple-element.31.x_ref), channel_id=1, source_target_pairs={{0,64},{128,192},{384,448},{480,416},{352,288},{96,32},{64,0},{192... | collective-permute-start | bytes 393224 | tf_op jit(solution)/shard_map/ppermute | solution.py:316
  67.1 10.5 %collective-permute-start.3 = (f32[128,256]{1,0:T(8,128)S(1)}, f32[128,256]{1,0:T(8,128)S(1)}, u32[]{:S(2)}, u32[]{:S(2)}) collective-permute-start(f32[128,256]{1,0:T(8,128)S(1)} %get-tuple-element.32.y_ref), channel_id=1, source_target_pairs={{64,128},{192,256},{320,384},{448,480},{416,352},{288,224},{160,96... | collective-permute-start | bytes 393224 | tf_op jit(solution)/shard_map/ppermute | solution.py:316
  71.1 6.9 %collective-permute-start.4 = (f32[128,256]{1,0:T(8,128)S(1)}, f32[128,256]{1,0:T(8,128)S(1)}, u32[]{:S(2)}, u32[]{:S(2)}) collective-permute-start(f32[128,256]{1,0:T(8,128)S(1)} %get-tuple-element.33.late_ref), channel_id=1, source_target_pairs={{256,320},{224,160},{320,256},{160,224},{257,321},{225,161},{321,2... | collective-permute-start | bytes 393224 | tf_op jit(solution)/shard_map/ppermute | solution.py:316

commit v6 on v5

--- a/solution.py
+++ b/solution.py
@@ -45,25 +45,21 @@
 def to_cycle(x):
     left, right = halves(x)
     lane = lanes_of(left)
-    up, down = 2 * lane % LANES, (2 * LANES - 1 - 2 * lane) % LANES
     first = lane < LANES // 2
-    return jnp.concatenate(
-        [
-            jnp.where(first, pick(left, up), pick(right, up)),
-            jnp.where(first, pick(right, down), pick(left, down)),
-        ],
-        axis=1,
-    )
+    evens_then_odds = jnp.where(first, 2 * lane, 2 * LANES - 1 - 2 * lane)
+    left = pick(left, evens_then_odds)
+    right = pltpu.roll(pick(right, evens_then_odds), LANES // 2, 1)
+    return jnp.concatenate([jnp.where(first, left, right), jnp.where(first, right, left)], axis=1)
 
 
 def from_cycle(x):
-    left, right = halves(x)
-    lane = lanes_of(left)
-    half = lane // 2
-    even = lane % 2 == 0
-    low = jnp.where(even, pick(left, half), pick(right, LANES - 1 - half))
-    high = jnp.where(even, pick(left, LANES // 2 + half), pick(right, LANES // 2 - 1 - half))
-    return jnp.concatenate([low, high], axis=1)
+    up, down = halves(x)
+    lane = lanes_of(up)
+    first = lane < LANES // 2
+    left = jnp.where(first, up, down)
+    right = pltpu.roll(jnp.where(first, down, up), LANES // 2, 1)
+    place = jnp.where(lane % 2 == 0, lane // 2, LANES - 1 - lane // 2)
+    return jnp.concatenate([pick(left, place), pick(right, place)], axis=1)
 
 
 def turn(ahead, back, matrix):
@@ -276,25 +272,36 @@
 
 
 def finish_kernel(
-    count, place_ref, top_before_ref, bottom_before_ref, top_after_ref, bottom_after_ref, parts_ref, out_ref
+    count, place_ref, top_before_ref, bottom_before_ref, top_after_ref, bottom_after_ref, parts_ref,
+    out_hbm, out_ref, sems
 ):
     place = place_ref[0, 0]
     both = three_matrices(ordered_sum(parts_ref))
     matrices_before, matrices_after = wide(both, 0), wide(both, 1)
-    for row in chunks(out_ref):
-        top, bottom = rotated(top_before_ref[row, :], bottom_before_ref[row, :], matrices_before)
-        out_ref[row, :HALF] = from_cycle(chosen(place == 1, reverse(bottom), top))
-        top, bottom = rotated(top_after_ref[row, :], bottom_after_ref[row, :], matrices_after)
-        out_ref[row, HALF:] = from_cycle(chosen(place == count - 1, top, reverse(bottom)))
-
-
-def call(kernel, inputs, outputs):
+    size = out_ref.shape[0] // sems.shape[0]
+    copies = []
+    for i in range(sems.shape[0]):
+        for start in range(i * size, (i + 1) * size, CHUNK):
+            row = pl.ds(start, CHUNK)
+            top, bottom = rotated(top_before_ref[row, :], bottom_before_ref[row, :], matrices_before)
+            out_ref[row, :HALF] = from_cycle(chosen(place == 1, reverse(bottom), top))
+            top, bottom = rotated(top_after_ref[row, :], bottom_after_ref[row, :], matrices_after)
+            out_ref[row, HALF:] = from_cycle(chosen(place == count - 1, top, reverse(bottom)))
+        part = pl.ds(i * size, size)
+        copies.append(pltpu.make_async_copy(out_ref.at[part], out_hbm.at[part], sems.at[i]))
+        copies[-1].start()
+    for copy in copies:
+        copy.wait()
+
+
+def call(kernel, inputs, outputs, scratch=(), space=pltpu.VMEM):
     spec = pl.BlockSpec(memory_space=pltpu.VMEM)
     return pl.pallas_call(
         kernel,
         in_specs=[pl.BlockSpec(memory_space=pltpu.SMEM)] + [spec] * (len(inputs) - 1),
-        out_specs=[spec] * len(outputs),
+        out_specs=[pl.BlockSpec(memory_space=space)] * len(outputs),
         out_shape=[jax.ShapeDtypeStruct(shape, jnp.float32) for shape in outputs],
+        scratch_shapes=list(scratch),
         compiler_params=pltpu.CompilerParams(vmem_limit_bytes=8 * 1024 * 1024),
     )(*inputs)
 
@@ -353,6 +360,8 @@
         functools.partial(finish_kernel, count),
         [place, *blocks, row_parts(band)],
         [(rows, 2 * HALF)],
+        [pltpu.VMEM((rows, 2 * HALF), jnp.float32), pltpu.SemaphoreType.DMA((4,))],
+        pltpu.HBM,
     )
     return out
 

time: 107 us -> 106 us (level)
  no operation moved by 1% of the time
where the time goes in v6:
time: 106 us
  blocking collectives  79.5 us (75%)
  starting transfers between devices  12.1 us (11%)
  waiting for transfers between devices  9.3 us (9%)
  Pallas kernels  3.59 us (3%)
    all_to_all x6, blocking collectives, from_all(): lax.all_to_all(copies, axes, 0, 0, tiled=True, axis_index_groups=groups)  79.5 us
    ppermute x5, starting transfers between devices, exchange(): return lax.ppermute(x, 'pair', edges + [(j, i) for i, j in edges])  12.1 us
    ppermute x5, waiting for transfers between devices, exchange(): return lax.ppermute(x, 'pair', edges + [(j, i) for i, j in edges])  9.3 us
    pallas_call x6, Pallas kernels, call(): pl.pallas_call(kernel, in_specs=[pl.BlockSpec(memory_space=pltpu.SMEM)] +...  3.59 us
  transfers between devices with their start and end apart: 5, of which 3 were waited for; matrix products, arithmetic and copies ran while one was open for 0% of the time, Pallas kernels for 0%

profile of v6, /device:TPU:4, one launch (start us, length us, event | category | flops | bytes accessed | tf_op | source)
XLA Modules:
  0.0 105.7 jit_solution(15751091072548864813)
XLA Ops:
  0.0 0.0 copy-start
  0.0 0.9 copy-done
  1.0 0.5 shard_map.17
  1.4 8.4 %all_to_all.30 = f32[4,24,128]{2,1,0:T(8,128)S(1)} all-to-all(f32[4,24,128]{2,1,0:T(8,128)S(1)} %broadcast_in_dim.18), channel_id=1, replica_groups=mesh['pair'=16,'half'=2,'far'=8,'near'=2] {'half','near'}, dimensions={0} | all-to-all | bytes 98304 | tf_op jit(solution)/shard_map/all_to_all | solution.py:314
  9.9 21.2 %all_to_all.31.parts_ref = f32[8,24,128]{2,1,0:T(8,128)S(1)} all-to-all(f32[8,24,128]{2,1,0:T(8,128)S(1)} %broadcast_in_dim.20), channel_id=1, replica_groups={{8,10,12,14,0,2,4,6},{9,11,13,15,1,3,5,7},{24,26,28,30,16,18,20,22},{25..., dimensions={0} | all-to-all | bytes 196608 | tf_op jit(solution)/shard_map/all_to_all | solution.py:314
  31.1 0.5 shard_map.18
  31.6 2.3 %collective-permute-start = (f32[128,256]{1,0:T(8,128)S(1)}, f32[128,256]{1,0:T(8,128)S(1)}, u32[]{:S(2)}, u32[]{:S(2)}) collective-permute-start(f32[128,256]{1,0:T(8,128)S(1)} %get-tuple-element.26), channel_id=1, source_target_pairs={{32,64},{96,128},{160,192},{224,256},{288,320},{352,384},{416,448}... | collective-permute-start | bytes 393224 | tf_op jit(solution)/shard_map/ppermute | solution.py:323
  33.8 3.2 %collective-permute-start.1 = (f32[128,256]{1,0:T(8,128)S(1)}, f32[128,256]{1,0:T(8,128)S(1)}, u32[]{:S(2)}, u32[]{:S(2)}) collective-permute-start(f32[128,256]{1,0:T(8,128)S(1)} %get-tuple-element.27), channel_id=1, source_target_pairs={{0,32},{64,96},{128,160},{192,224},{256,288},{320,352},{384,416},{... | collective-permute-start | bytes 393224 | tf_op jit(solution)/shard_map/ppermute | solution.py:323
  37.1 4.4 %collective-permute-done.odd_ref = f32[128,256]{1,0:T(8,128)S(1)} collective-permute-done((f32[128,256]{1,0:T(8,128)S(1)}, f32[128,256]{1,0:T(8,128)S(1)}, u32[]{:S(2)}, u32[]{:S(2)}) %collective-permute-start) | collective-permute-done | bytes 131104 | tf_op jit(solution)/shard_map/ppermute | solution.py:323
  41.5 0.0 collective-permute-done.1.even_ref
  41.5 0.2 shard_map.19
  41.7 7.2 %all_to_all.32 = f32[4,24,128]{2,1,0:T(8,128)S(1)} all-to-all(f32[4,24,128]{2,1,0:T(8,128)S(1)} %broadcast_in_dim.21), channel_id=1, replica_groups=mesh['pair'=16,'half'=2,'far'=8,'near'=2] {'half','near'}, dimensions={0} | all-to-all | bytes 98304 | tf_op jit(solution)/shard_map/all_to_all | solution.py:314
  48.9 16.3 %all_to_all.33.parts_ref = f32[8,24,128]{2,1,0:T(8,128)S(1)} all-to-all(f32[8,24,128]{2,1,0:T(8,128)S(1)} %broadcast_in_dim.23), channel_id=1, replica_groups={{8,10,12,14,0,2,4,6},{9,11,13,15,1,3,5,7},{24,26,28,30,16,18,20,22},{25..., dimensions={0} | all-to-all | bytes 196608 | tf_op jit(solution)/shard_map/all_to_all | solution.py:314
  65.2 0.5 shard_map.20
  65.7 0.7 collective-permute-start.2
  66.4 4.0 %collective-permute-start.3 = (f32[128,256]{1,0:T(8,128)S(1)}, f32[128,256]{1,0:T(8,128)S(1)}, u32[]{:S(2)}, u32[]{:S(2)}) collective-permute-start(f32[128,256]{1,0:T(8,128)S(1)} %get-tuple-element.32.y_ref), channel_id=1, source_target_pairs={{64,128},{192,256},{320,384},{448,480},{416,352},{288,224},{160,96... | collective-permute-start | bytes 393224 | tf_op jit(solution)/shard_map/ppermute | solution.py:323
  70.4 1.9 %collective-permute-start.4 = (f32[128,256]{1,0:T(8,128)S(1)}, f32[128,256]{1,0:T(8,128)S(1)}, u32[]{:S(2)}, u32[]{:S(2)}) collective-permute-start(f32[128,256]{1,0:T(8,128)S(1)} %get-tuple-element.33.late_ref), channel_id=1, source_target_pairs={{256,320},{224,160},{320,256},{160,224},{257,321},{225,161},{321,2... | collective-permute-start | bytes 393224 | tf_op jit(solution)/shard_map/ppermute | solution.py:323
  72.3 0.0 collective-permute-done.2.x_in_ref
  72.3 4.5 %collective-permute-done.3.y_in_ref = f32[128,256]{1,0:T(8,128)S(1)} collective-permute-done((f32[128,256]{1,0:T(8,128)S(1)}, f32[128,256]{1,0:T(8,128)S(1)}, u32[]{:S(2)}, u32[]{:S(2)}) %collective-permute-start.3) | collective-permute-done | bytes 131104 | tf_op jit(solution)/shard_map/ppermute | solution.py:323
  76.9 0.4 collective-permute-done.4.late_in_ref
  77.3 0.4 shard_map.21
  77.7 7.8 %all_to_all.34 = f32[4,48,128]{2,1,0:T(8,128)S(1)} all-to-all(f32[4,48,128]{2,1,0:T(8,128)S(1)} %broadcast_in_dim.48), channel_id=1, replica_groups=mesh['pair'=16,'half'=2,'far'=8,'near'=2] {'half','near'}, dimensions={0} | all-to-all | bytes 196608 | tf_op jit(solution)/shard_map/all_to_all | solution.py:314
  85.6 18.6 %all_to_all.35.parts_ref = f32[8,48,128]{2,1,0:T(8,128)S(1)} all-to-all(f32[8,48,128]{2,1,0:T(8,128)S(1)} %broadcast_in_dim.50), channel_id=1, replica_groups={{8,10,12,14,0,2,4,6},{9,11,13,15,1,3,5,7},{24,26,28,30,16,18,20,22},{25..., dimensions={0} | all-to-all | bytes 393216 | tf_op jit(solution)/shard_map/all_to_all | solution.py:314
  104.1 1.5 %shard_map.22 = f32[128,512]{1,0:T(8,128)} custom-call(s32[1,1]{1,0:T(1,128)} %bitcast.place_ref, f32[128,256]{1,0:T(8,128)S(1)} %get-tuple-element.34.top_before_ref, f32[128,256]{1,0:T(8,128)S(1)} %get-tuple-element.35.bottom_before_ref, f32[128,256]{1,0:T(8,128)S(1)} %get-tuple-element.36.top_after_ref, ...), custom_call_target="tpu_custom_call" | custom-call | tf_op jit(solution)/shard_map/pallas_call | solution.py:299
  (9 shorter events, 0.1 us)
Async XLA Ops:
  0.0 0.9 copy-start
  31.6 9.9 %collective-permute-start = (f32[128,256]{1,0:T(8,128)S(1)}, f32[128,256]{1,0:T(8,128)S(1)}, u32[]{:S(2)}, u32[]{:S(2)}) collective-permute-start(f32[128,256]{1,0:T(8,128)S(1)} %get-tuple-element.26), channel_id=1, source_target_pairs={{32,64},{96,128},{160,192},{224,256},{288,320},{352,384},{416,448}... | collective-permute-start | bytes 393224 | tf_op jit(solution)/shard_map/ppermute | solution.py:323
  33.8 7.6 %collective-permute-start.1 = (f32[128,256]{1,0:T(8,128)S(1)}, f32[128,256]{1,0:T(8,128)S(1)}, u32[]{:S(2)}, u32[]{:S(2)}) collective-permute-start(f32[128,256]{1,0:T(8,128)S(1)} %get-tuple-element.27), channel_id=1, source_target_pairs={{0,32},{64,96},{128,160},{192,224},{256,288},{320,352},{384,416},{... | collective-permute-start | bytes 393224 | tf_op jit(solution)/shard_map/ppermute | solution.py:323
  65.7 6.6 %collective-permute-start.2 = (f32[128,256]{1,0:T(8,128)S(1)}, f32[128,256]{1,0:T(8,128)S(1)}, u32[]{:S(2)}, u32[]{:S(2)}) collective-permute-start(f32[128,256]{1,0:T(8,128)S(1)} %get-tuple-element.31.x_ref), channel_id=1, source_target_pairs={{0,64},{128,192},{384,448},{480,416},{352,288},{96,32},{64,0},{192... | collective-permute-start | bytes 393224 | tf_op jit(solution)/shard_map/ppermute | solution.py:323
  66.4 10.5 %collective-permute-start.3 = (f32[128,256]{1,0:T(8,128)S(1)}, f32[128,256]{1,0:T(8,128)S(1)}, u32[]{:S(2)}, u32[]{:S(2)}) collective-permute-start(f32[128,256]{1,0:T(8,128)S(1)} %get-tuple-element.32.y_ref), channel_id=1, source_target_pairs={{64,128},{192,256},{320,384},{448,480},{416,352},{288,224},{160,96... | collective-permute-start | bytes 393224 | tf_op jit(solution)/shard_map/ppermute | solution.py:323
  70.4 6.9 %collective-permute-start.4 = (f32[128,256]{1,0:T(8,128)S(1)}, f32[128,256]{1,0:T(8,128)S(1)}, u32[]{:S(2)}, u32[]{:S(2)}) collective-permute-start(f32[128,256]{1,0:T(8,128)S(1)} %get-tuple-element.33.late_ref), channel_id=1, source_target_pairs={{256,320},{224,160},{320,256},{160,224},{257,321},{225,161},{321,2... | collective-permute-start | bytes 393224 | tf_op jit(solution)/shard_map/ppermute | solution.py:323

commit v7 on v6

--- a/solution.py
+++ b/solution.py
@@ -180,8 +180,18 @@
     return [pl.ds(start, CHUNK) for start in range(0, ref.shape[0], CHUNK)]
 
 
-def start_kernel(place_ref, work_ref, top_ref, bottom_ref, band_ref):
+def start_kernel(place_ref, work_hbm, top_ref, bottom_ref, band_ref, work_ref, sems):
+    rows = work_ref.shape[0]
+    size = rows // sems.shape[0]
+    copies = []
+    for i in range(sems.shape[0]):
+        part = pl.ds(i * size, size)
+        copies.append(pltpu.make_async_copy(work_hbm.at[part], work_ref.at[part], sems.at[i]))
+        copies[-1].start()
+
     def read(start):
+        if start % size == 0:
+            copies[start // size].wait()
         row = pl.ds(start, CHUNK)
         top = to_cycle(work_ref[row, :HALF])
         bottom = reverse(to_cycle(work_ref[row, HALF:]))
@@ -189,7 +199,7 @@
         bottom_ref[row, :] = bottom
         return top, bottom
 
-    band_ref[...] = pack(bands_of(read, work_ref.shape[0]))
+    band_ref[...] = pack(bands_of(read, rows))
 
 
 def rotate_kernel(place_ref, top_ref, bottom_ref, parts_ref, kept_ref, odd_ref, even_ref):
@@ -294,15 +304,14 @@
         copy.wait()
 
 
-def call(kernel, inputs, outputs, scratch=(), space=pltpu.VMEM):
-    spec = pl.BlockSpec(memory_space=pltpu.VMEM)
+def call(kernel, inputs, outputs, scratch=(), source=pltpu.VMEM, target=pltpu.VMEM, limit=8):
     return pl.pallas_call(
         kernel,
-        in_specs=[pl.BlockSpec(memory_space=pltpu.SMEM)] + [spec] * (len(inputs) - 1),
-        out_specs=[pl.BlockSpec(memory_space=space)] * len(outputs),
+        in_specs=[pl.BlockSpec(memory_space=pltpu.SMEM)] + [pl.BlockSpec(memory_space=source)] * (len(inputs) - 1),
+        out_specs=[pl.BlockSpec(memory_space=target)] * len(outputs),
         out_shape=[jax.ShapeDtypeStruct(shape, jnp.float32) for shape in outputs],
         scratch_shapes=list(scratch),
-        compiler_params=pltpu.CompilerParams(vmem_limit_bytes=8 * 1024 * 1024),
+        compiler_params=pltpu.CompilerParams(vmem_limit_bytes=limit * 1024 * 1024),
     )(*inputs)
 
 
@@ -334,7 +343,14 @@
     x_edges = list(zip(cycle[::2], cycle[1::2]))
     y_edges = list(zip(cycle[1::2], cycle[2::2] + cycle[:1]))
 
-    top, bottom, band = call(start_kernel, [place, snapshots], [block, block, packed])
+    top, bottom, band = call(
+        start_kernel,
+        [place, snapshots],
+        [block, block, packed],
+        [pltpu.VMEM((rows, 2 * HALF), jnp.float32), pltpu.SemaphoreType.DMA((4,))],
+        source=pltpu.HBM,
+        limit=60,
+    )
     kept, odd, even = call(
         rotate_kernel, [place, top, bottom, row_parts(band)], [block] * 3
     )
@@ -361,7 +377,7 @@
         [place, *blocks, row_parts(band)],
         [(rows, 2 * HALF)],
         [pltpu.VMEM((rows, 2 * HALF), jnp.float32), pltpu.SemaphoreType.DMA((4,))],
-        pltpu.HBM,
+        target=pltpu.HBM,
     )
     return out
 

time: 106 us -> 108 us (1.019)
  Pallas kernels: 3.59 us -> 5.58 us
    pallas_call x6, Pallas kernels: 3.59 us -> 5.58 us  [call(): pl.pallas_call(kernel, in_specs=[pl.BlockSpec(memory_space=pltpu.SMEM)] +...]
where the time goes in v7:
time: 108 us
  blocking collectives  79.7 us (74%)
  starting transfers between devices  12.1 us (11%)
  waiting for transfers between devices  9.3 us (9%)
  Pallas kernels  5.58 us (5%)
    all_to_all x6, blocking collectives, from_all(): lax.all_to_all(copies, axes, 0, 0, tiled=True, axis_index_groups=groups)  79.7 us
    ppermute x5, starting transfers between devices, exchange(): return lax.ppermute(x, 'pair', edges + [(j, i) for i, j in edges])  12.1 us
    ppermute x5, waiting for transfers between devices, exchange(): return lax.ppermute(x, 'pair', edges + [(j, i) for i, j in edges])  9.3 us
    pallas_call x6, Pallas kernels, call(): pl.pallas_call(kernel, in_specs=[pl.BlockSpec(memory_space=pltpu.SMEM)] +...  5.58 us
  transfers between devices with their start and end apart: 5, of which 3 were waited for; matrix products, arithmetic and copies ran while one was open for 0% of the time, Pallas kernels for 0%

profile of v7, /device:TPU:4, one launch (start us, length us, event | category | flops | bytes accessed | tf_op | source)
XLA Modules:
  0.0 107.6 jit_solution(11825284939546804943)
XLA Ops:
  0.0 2.5 %shard_map.17 = (f32[128,256]{1,0:T(8,128)}, f32[128,256]{1,0:T(8,128)}, f32[24,128]{1,0:T(8,128)}) custom-call(s32[1,1]{1,0:T(1,128)} %bitcast.place_ref, f32[128,512]{1,0:T(8,128)} %work_hbm.1), custom_call_target="tpu_custom_call" | custom-call | tf_op jit(solution)/shard_map/pallas_call | solution.py:308
  2.5 0.7 broadcast_in_dim.18
  3.2 8.4 %all_to_all.30 = f32[4,24,128]{2,1,0:T(8,128)S(1)} all-to-all(f32[4,24,128]{2,1,0:T(8,128)S(1)} %broadcast_in_dim.18), channel_id=1, replica_groups=mesh['pair'=16,'half'=2,'far'=8,'near'=2] {'half','near'}, dimensions={0} | all-to-all | bytes 98304 | tf_op jit(solution)/shard_map/all_to_all | solution.py:323
  11.6 0.0 copy-start
  11.6 0.0 copy-start.1
  11.6 21.3 %all_to_all.31.parts_ref = f32[8,24,128]{2,1,0:T(8,128)S(1)} all-to-all(f32[8,24,128]{2,1,0:T(8,128)S(1)} %broadcast_in_dim.20), channel_id=1, replica_groups={{8,10,12,14,0,2,4,6},{9,11,13,15,1,3,5,7},{24,26,28,30,16,18,20,22},{25..., dimensions={0} | all-to-all | bytes 196608 | tf_op jit(solution)/shard_map/all_to_all | solution.py:323
  32.9 0.0 copy-done
  32.9 0.0 copy-done.1
  32.9 0.5 shard_map.18
  33.4 2.3 %collective-permute-start = (f32[128,256]{1,0:T(8,128)S(1)}, f32[128,256]{1,0:T(8,128)S(1)}, u32[]{:S(2)}, u32[]{:S(2)}) collective-permute-start(f32[128,256]{1,0:T(8,128)S(1)} %get-tuple-element.26), channel_id=1, source_target_pairs={{32,64},{96,128},{160,192},{224,256},{288,320},{352,384},{416,448}... | collective-permute-start | bytes 393224 | tf_op jit(solution)/shard_map/ppermute | solution.py:332
  35.7 3.2 %collective-permute-start.1 = (f32[128,256]{1,0:T(8,128)S(1)}, f32[128,256]{1,0:T(8,128)S(1)}, u32[]{:S(2)}, u32[]{:S(2)}) collective-permute-start(f32[128,256]{1,0:T(8,128)S(1)} %get-tuple-element.27), channel_id=1, source_target_pairs={{0,32},{64,96},{128,160},{192,224},{256,288},{320,352},{384,416},{... | collective-permute-start | bytes 393224 | tf_op jit(solution)/shard_map/ppermute | solution.py:332
  39.0 4.4 %collective-permute-done.odd_ref = f32[128,256]{1,0:T(8,128)S(1)} collective-permute-done((f32[128,256]{1,0:T(8,128)S(1)}, f32[128,256]{1,0:T(8,128)S(1)}, u32[]{:S(2)}, u32[]{:S(2)}) %collective-permute-start) | collective-permute-done | bytes 131104 | tf_op jit(solution)/shard_map/ppermute | solution.py:332
  43.3 0.0 collective-permute-done.1.even_ref
  43.3 0.2 shard_map.19
  43.6 7.2 %all_to_all.32 = f32[4,24,128]{2,1,0:T(8,128)S(1)} all-to-all(f32[4,24,128]{2,1,0:T(8,128)S(1)} %broadcast_in_dim.21), channel_id=1, replica_groups=mesh['pair'=16,'half'=2,'far'=8,'near'=2] {'half','near'}, dimensions={0} | all-to-all | bytes 98304 | tf_op jit(solution)/shard_map/all_to_all | solution.py:323
  50.8 16.3 %all_to_all.33.parts_ref = f32[8,24,128]{2,1,0:T(8,128)S(1)} all-to-all(f32[8,24,128]{2,1,0:T(8,128)S(1)} %broadcast_in_dim.23), channel_id=1, replica_groups={{8,10,12,14,0,2,4,6},{9,11,13,15,1,3,5,7},{24,26,28,30,16,18,20,22},{25..., dimensions={0} | all-to-all | bytes 196608 | tf_op jit(solution)/shard_map/all_to_all | solution.py:323
  67.1 0.5 shard_map.20
  67.6 0.7 collective-permute-start.2
  68.3 4.0 %collective-permute-start.3 = (f32[128,256]{1,0:T(8,128)S(1)}, f32[128,256]{1,0:T(8,128)S(1)}, u32[]{:S(2)}, u32[]{:S(2)}) collective-permute-start(f32[128,256]{1,0:T(8,128)S(1)} %get-tuple-element.32.y_ref), channel_id=1, source_target_pairs={{64,128},{192,256},{320,384},{448,480},{416,352},{288,224},{160,96... | collective-permute-start | bytes 393224 | tf_op jit(solution)/shard_map/ppermute | solution.py:332
  72.3 1.9 %collective-permute-start.4 = (f32[128,256]{1,0:T(8,128)S(1)}, f32[128,256]{1,0:T(8,128)S(1)}, u32[]{:S(2)}, u32[]{:S(2)}) collective-permute-start(f32[128,256]{1,0:T(8,128)S(1)} %get-tuple-element.33.late_ref), channel_id=1, source_target_pairs={{256,320},{224,160},{320,256},{160,224},{257,321},{225,161},{321,2... | collective-permute-start | bytes 393224 | tf_op jit(solution)/shard_map/ppermute | solution.py:332
  74.2 0.0 collective-permute-done.2.x_in_ref
  74.2 4.5 %collective-permute-done.3.y_in_ref = f32[128,256]{1,0:T(8,128)S(1)} collective-permute-done((f32[128,256]{1,0:T(8,128)S(1)}, f32[128,256]{1,0:T(8,128)S(1)}, u32[]{:S(2)}, u32[]{:S(2)}) %collective-permute-start.3) | collective-permute-done | bytes 131104 | tf_op jit(solution)/shard_map/ppermute | solution.py:332
  78.8 0.4 collective-permute-done.4.late_in_ref
  79.1 0.4 shard_map.21
  79.6 7.8 %all_to_all.34 = f32[4,48,128]{2,1,0:T(8,128)S(1)} all-to-all(f32[4,48,128]{2,1,0:T(8,128)S(1)} %broadcast_in_dim.48), channel_id=1, replica_groups=mesh['pair'=16,'half'=2,'far'=8,'near'=2] {'half','near'}, dimensions={0} | all-to-all | bytes 196608 | tf_op jit(solution)/shard_map/all_to_all | solution.py:323
  87.4 18.6 %all_to_all.35.parts_ref = f32[8,48,128]{2,1,0:T(8,128)S(1)} all-to-all(f32[8,48,128]{2,1,0:T(8,128)S(1)} %broadcast_in_dim.50), channel_id=1, replica_groups={{8,10,12,14,0,2,4,6},{9,11,13,15,1,3,5,7},{24,26,28,30,16,18,20,22},{25..., dimensions={0} | all-to-all | bytes 393216 | tf_op jit(solution)/shard_map/all_to_all | solution.py:323
  106.0 1.5 %shard_map.22 = f32[128,512]{1,0:T(8,128)} custom-call(s32[1,1]{1,0:T(1,128)} %bitcast.place_ref, f32[128,256]{1,0:T(8,128)S(1)} %get-tuple-element.34.top_before_ref, f32[128,256]{1,0:T(8,128)S(1)} %get-tuple-element.35.bottom_before_ref, f32[128,256]{1,0:T(8,128)S(1)} %get-tuple-element.36.top_after_ref, ...), custom_call_target="tpu_custom_call" | custom-call | tf_op jit(solution)/shard_map/pallas_call | solution.py:308
  (8 shorter events, 0.1 us)
Async XLA Ops:
  11.6 21.3 %copy-start = (f32[128,256]{1,0:T(8,128)S(1)}, f32[128,256]{1,0:T(8,128)}, u32[]{:S(2)}) copy-start(f32[128,256]{1,0:T(8,128)} %get-tuple-element.22.top_ref) | copy-start | bytes 393220
  11.6 21.3 %copy-start.1 = (f32[128,256]{1,0:T(8,128)S(1)}, f32[128,256]{1,0:T(8,128)}, u32[]{:S(2)}) copy-start(f32[128,256]{1,0:T(8,128)} %get-tuple-element.23.bottom_ref) | copy-start | bytes 393220
  33.4 9.9 %collective-permute-start = (f32[128,256]{1,0:T(8,128)S(1)}, f32[128,256]{1,0:T(8,128)S(1)}, u32[]{:S(2)}, u32[]{:S(2)}) collective-permute-start(f32[128,256]{1,0:T(8,128)S(1)} %get-tuple-element.26), channel_id=1, source_target_pairs={{32,64},{96,128},{160,192},{224,256},{288,320},{352,384},{416,448}... | collective-permute-start | bytes 393224 | tf_op jit(solution)/shard_map/ppermute | solution.py:332
  35.7 7.6 %collective-permute-start.1 = (f32[128,256]{1,0:T(8,128)S(1)}, f32[128,256]{1,0:T(8,128)S(1)}, u32[]{:S(2)}, u32[]{:S(2)}) collective-permute-start(f32[128,256]{1,0:T(8,128)S(1)} %get-tuple-element.27), channel_id=1, source_target_pairs={{0,32},{64,96},{128,160},{192,224},{256,288},{320,352},{384,416},{... | collective-permute-start | bytes 393224 | tf_op jit(solution)/shard_map/ppermute | solution.py:332
  67.6 6.6 %collective-permute-start.2 = (f32[128,256]{1,0:T(8,128)S(1)}, f32[128,256]{1,0:T(8,128)S(1)}, u32[]{:S(2)}, u32[]{:S(2)}) collective-permute-start(f32[128,256]{1,0:T(8,128)S(1)} %get-tuple-element.31.x_ref), channel_id=1, source_target_pairs={{0,64},{128,192},{384,448},{480,416},{352,288},{96,32},{64,0},{192... | collective-permute-start | bytes 393224 | tf_op jit(solution)/shard_map/ppermute | solution.py:332
  68.3 10.5 %collective-permute-start.3 = (f32[128,256]{1,0:T(8,128)S(1)}, f32[128,256]{1,0:T(8,128)S(1)}, u32[]{:S(2)}, u32[]{:S(2)}) collective-permute-start(f32[128,256]{1,0:T(8,128)S(1)} %get-tuple-element.32.y_ref), channel_id=1, source_target_pairs={{64,128},{192,256},{320,384},{448,480},{416,352},{288,224},{160,96... | collective-permute-start | bytes 393224 | tf_op jit(solution)/shard_map/ppermute | solution.py:332
  72.3 6.9 %collective-permute-start.4 = (f32[128,256]{1,0:T(8,128)S(1)}, f32[128,256]{1,0:T(8,128)S(1)}, u32[]{:S(2)}, u32[]{:S(2)}) collective-permute-start(f32[128,256]{1,0:T(8,128)S(1)} %get-tuple-element.33.late_ref), channel_id=1, source_target_pairs={{256,320},{224,160},{320,256},{160,224},{257,321},{225,161},{321,2... | collective-permute-start | bytes 393224 | tf_op jit(solution)/shard_map/ppermute | solution.py:332

commit v8 on v6

--- a/solution.py
+++ b/solution.py
@@ -316,7 +316,7 @@
 
 def row_parts(x):
     near = ordered_sum(from_all(x, ("half", "near")))
-    return from_all(near, "far", lax.axis_size("far") // 2)
+    return from_all(near, "far", lax.axis_size("far") // 2 + 1)
 
 
 def exchange(x, edges):

time: 106 us -> 106 us (level)
  no operation moved by 1% of the time
where the time goes in v8:
time: 106 us
  blocking collectives  79.6 us (75%)
  starting transfers between devices  12.2 us (12%)
  waiting for transfers between devices  9.3 us (9%)
  Pallas kernels  3.59 us (3%)
    all_to_all x6, blocking collectives, from_all(): lax.all_to_all(copies, axes, 0, 0, tiled=True, axis_index_groups=groups)  79.6 us
    ppermute x5, starting transfers between devices, exchange(): return lax.ppermute(x, 'pair', edges + [(j, i) for i, j in edges])  12.2 us
    ppermute x5, waiting for transfers between devices, exchange(): return lax.ppermute(x, 'pair', edges + [(j, i) for i, j in edges])  9.3 us
    pallas_call x6, Pallas kernels, call(): pl.pallas_call(kernel, in_specs=[pl.BlockSpec(memory_space=pltpu.SMEM)] +...  3.59 us
  transfers between devices with their start and end apart: 5, of which 3 were waited for; matrix products, arithmetic and copies ran while one was open for 0% of the time, Pallas kernels for 0%

profile of v8, /device:TPU:4, one launch (start us, length us, event | category | flops | bytes accessed | tf_op | source)
XLA Modules:
  0.0 105.8 jit_solution(4659242926172297991)
XLA Ops:
  0.0 0.0 copy-start
  0.0 0.9 copy-done
  1.0 0.5 shard_map.17
  1.4 8.4 %all_to_all.30 = f32[4,24,128]{2,1,0:T(8,128)S(1)} all-to-all(f32[4,24,128]{2,1,0:T(8,128)S(1)} %broadcast_in_dim.18), channel_id=1, replica_groups=mesh['pair'=16,'half'=2,'far'=8,'near'=2] {'half','near'}, dimensions={0} | all-to-all | bytes 98304 | tf_op jit(solution)/shard_map/all_to_all | solution.py:314
  9.9 21.6 %all_to_all.31.parts_ref = f32[8,24,128]{2,1,0:T(8,128)S(1)} all-to-all(f32[8,24,128]{2,1,0:T(8,128)S(1)} %broadcast_in_dim.20), channel_id=1, replica_groups={{10,12,14,0,2,4,6,8},{11,13,15,1,3,5,7,9},{26,28,30,16,18,20,22,24},{27..., dimensions={0} | all-to-all | bytes 196608 | tf_op jit(solution)/shard_map/all_to_all | solution.py:314
  31.5 0.5 shard_map.18
  32.0 1.9 %collective-permute-start = (f32[128,256]{1,0:T(8,128)S(1)}, f32[128,256]{1,0:T(8,128)S(1)}, u32[]{:S(2)}, u32[]{:S(2)}) collective-permute-start(f32[128,256]{1,0:T(8,128)S(1)} %get-tuple-element.26), channel_id=1, source_target_pairs={{32,64},{96,128},{160,192},{224,256},{288,320},{352,384},{416,448}... | collective-permute-start | bytes 393224 | tf_op jit(solution)/shard_map/ppermute | solution.py:323
  33.9 3.6 %collective-permute-start.1 = (f32[128,256]{1,0:T(8,128)S(1)}, f32[128,256]{1,0:T(8,128)S(1)}, u32[]{:S(2)}, u32[]{:S(2)}) collective-permute-start(f32[128,256]{1,0:T(8,128)S(1)} %get-tuple-element.27), channel_id=1, source_target_pairs={{0,32},{64,96},{128,160},{192,224},{256,288},{320,352},{384,416},{... | collective-permute-start | bytes 393224 | tf_op jit(solution)/shard_map/ppermute | solution.py:323
  37.5 4.4 %collective-permute-done.odd_ref = f32[128,256]{1,0:T(8,128)S(1)} collective-permute-done((f32[128,256]{1,0:T(8,128)S(1)}, f32[128,256]{1,0:T(8,128)S(1)}, u32[]{:S(2)}, u32[]{:S(2)}) %collective-permute-start) | collective-permute-done | bytes 131104 | tf_op jit(solution)/shard_map/ppermute | solution.py:323
  41.9 0.0 collective-permute-done.1.even_ref
  41.9 0.2 shard_map.19
  42.2 7.2 %all_to_all.32 = f32[4,24,128]{2,1,0:T(8,128)S(1)} all-to-all(f32[4,24,128]{2,1,0:T(8,128)S(1)} %broadcast_in_dim.21), channel_id=1, replica_groups=mesh['pair'=16,'half'=2,'far'=8,'near'=2] {'half','near'}, dimensions={0} | all-to-all | bytes 98304 | tf_op jit(solution)/shard_map/all_to_all | solution.py:314
  49.3 16.2 %all_to_all.33.parts_ref = f32[8,24,128]{2,1,0:T(8,128)S(1)} all-to-all(f32[8,24,128]{2,1,0:T(8,128)S(1)} %broadcast_in_dim.23), channel_id=1, replica_groups={{10,12,14,0,2,4,6,8},{11,13,15,1,3,5,7,9},{26,28,30,16,18,20,22,24},{27..., dimensions={0} | all-to-all | bytes 196608 | tf_op jit(solution)/shard_map/all_to_all | solution.py:314
  65.5 0.5 shard_map.20
  66.0 0.7 collective-permute-start.2
  66.7 4.1 %collective-permute-start.3 = (f32[128,256]{1,0:T(8,128)S(1)}, f32[128,256]{1,0:T(8,128)S(1)}, u32[]{:S(2)}, u32[]{:S(2)}) collective-permute-start(f32[128,256]{1,0:T(8,128)S(1)} %get-tuple-element.32.y_ref), channel_id=1, source_target_pairs={{64,128},{192,256},{320,384},{448,480},{416,352},{288,224},{160,96... | collective-permute-start | bytes 393224 | tf_op jit(solution)/shard_map/ppermute | solution.py:323
  70.8 1.9 %collective-permute-start.4 = (f32[128,256]{1,0:T(8,128)S(1)}, f32[128,256]{1,0:T(8,128)S(1)}, u32[]{:S(2)}, u32[]{:S(2)}) collective-permute-start(f32[128,256]{1,0:T(8,128)S(1)} %get-tuple-element.33.late_ref), channel_id=1, source_target_pairs={{256,320},{224,160},{320,256},{160,224},{257,321},{225,161},{321,2... | collective-permute-start | bytes 393224 | tf_op jit(solution)/shard_map/ppermute | solution.py:323
  72.7 0.0 collective-permute-done.2.x_in_ref
  72.7 4.4 %collective-permute-done.3.y_in_ref = f32[128,256]{1,0:T(8,128)S(1)} collective-permute-done((f32[128,256]{1,0:T(8,128)S(1)}, f32[128,256]{1,0:T(8,128)S(1)}, u32[]{:S(2)}, u32[]{:S(2)}) %collective-permute-start.3) | collective-permute-done | bytes 131104 | tf_op jit(solution)/shard_map/ppermute | solution.py:323
  77.2 0.5 collective-permute-done.4.late_in_ref
  77.7 0.4 shard_map.21
  78.1 7.3 %all_to_all.34 = f32[4,48,128]{2,1,0:T(8,128)S(1)} all-to-all(f32[4,48,128]{2,1,0:T(8,128)S(1)} %broadcast_in_dim.48), channel_id=1, replica_groups=mesh['pair'=16,'half'=2,'far'=8,'near'=2] {'half','near'}, dimensions={0} | all-to-all | bytes 196608 | tf_op jit(solution)/shard_map/all_to_all | solution.py:314
  85.4 18.9 %all_to_all.35.parts_ref = f32[8,48,128]{2,1,0:T(8,128)S(1)} all-to-all(f32[8,48,128]{2,1,0:T(8,128)S(1)} %broadcast_in_dim.50), channel_id=1, replica_groups={{10,12,14,0,2,4,6,8},{11,13,15,1,3,5,7,9},{26,28,30,16,18,20,22,24},{27..., dimensions={0} | all-to-all | bytes 393216 | tf_op jit(solution)/shard_map/all_to_all | solution.py:314
  104.3 1.5 %shard_map.22 = f32[128,512]{1,0:T(8,128)} custom-call(s32[1,1]{1,0:T(1,128)} %bitcast.place_ref, f32[128,256]{1,0:T(8,128)S(1)} %get-tuple-element.34.top_before_ref, f32[128,256]{1,0:T(8,128)S(1)} %get-tuple-element.35.bottom_before_ref, f32[128,256]{1,0:T(8,128)S(1)} %get-tuple-element.36.top_after_ref, ...), custom_call_target="tpu_custom_call" | custom-call | tf_op jit(solution)/shard_map/pallas_call | solution.py:299
  (9 shorter events, 0.1 us)
Async XLA Ops:
  0.0 0.9 copy-start
  32.0 9.9 %collective-permute-start = (f32[128,256]{1,0:T(8,128)S(1)}, f32[128,256]{1,0:T(8,128)S(1)}, u32[]{:S(2)}, u32[]{:S(2)}) collective-permute-start(f32[128,256]{1,0:T(8,128)S(1)} %get-tuple-element.26), channel_id=1, source_target_pairs={{32,64},{96,128},{160,192},{224,256},{288,320},{352,384},{416,448}... | collective-permute-start | bytes 393224 | tf_op jit(solution)/shard_map/ppermute | solution.py:323
  33.9 8.0 %collective-permute-start.1 = (f32[128,256]{1,0:T(8,128)S(1)}, f32[128,256]{1,0:T(8,128)S(1)}, u32[]{:S(2)}, u32[]{:S(2)}) collective-permute-start(f32[128,256]{1,0:T(8,128)S(1)} %get-tuple-element.27), channel_id=1, source_target_pairs={{0,32},{64,96},{128,160},{192,224},{256,288},{320,352},{384,416},{... | collective-permute-start | bytes 393224 | tf_op jit(solution)/shard_map/ppermute | solution.py:323
  66.0 6.7 %collective-permute-start.2 = (f32[128,256]{1,0:T(8,128)S(1)}, f32[128,256]{1,0:T(8,128)S(1)}, u32[]{:S(2)}, u32[]{:S(2)}) collective-permute-start(f32[128,256]{1,0:T(8,128)S(1)} %get-tuple-element.31.x_ref), channel_id=1, source_target_pairs={{0,64},{128,192},{384,448},{480,416},{352,288},{96,32},{64,0},{192... | collective-permute-start | bytes 393224 | tf_op jit(solution)/shard_map/ppermute | solution.py:323
  66.7 10.5 %collective-permute-start.3 = (f32[128,256]{1,0:T(8,128)S(1)}, f32[128,256]{1,0:T(8,128)S(1)}, u32[]{:S(2)}, u32[]{:S(2)}) collective-permute-start(f32[128,256]{1,0:T(8,128)S(1)} %get-tuple-element.32.y_ref), channel_id=1, source_target_pairs={{64,128},{192,256},{320,384},{448,480},{416,352},{288,224},{160,96... | collective-permute-start | bytes 393224 | tf_op jit(solution)/shard_map/ppermute | solution.py:323
  70.8 6.9 %collective-permute-start.4 = (f32[128,256]{1,0:T(8,128)S(1)}, f32[128,256]{1,0:T(8,128)S(1)}, u32[]{:S(2)}, u32[]{:S(2)}) collective-permute-start(f32[128,256]{1,0:T(8,128)S(1)} %get-tuple-element.33.late_ref), channel_id=1, source_target_pairs={{256,320},{224,160},{320,256},{160,224},{257,321},{225,161},{321,2... | collective-permute-start | bytes 393224 | tf_op jit(solution)/shard_map/ppermute | solution.py:323
